TPU v7x, 512 devices: a whole 4x4x16 slice. The times are simulated.
512 devices in a mesh: aa: 16 (over z_hi, y), ba: 4 (over x), col: 8 (over z_lo, core).
Axes of the slice: x: 4, y: 4, z: 16 (z_hi: 4, z_lo: 4; z = z_hi * 4 + z_lo), core: 2. Of those that a mesh axis runs over, the one named last changes fastest.
Arguments:
- field: float32 [512, 128, 4096], P('aa', 'ba', 'col'), may hold values from -85 to 85
- factor: float32 [512, 256], P('aa'), may hold values from -0.25 to 0.25
Outputs:
- gram: float32 [512, 512], P('aa')
- truncated: float32 [256, 128, 4096], P('aa', 'ba', 'col')
All inputs are finite; a program needn't handle non-finite values.
Results may differ from a plain program's by a relative error of at most 0.00011.
Values sent between devices are 32-bit elements; how exact they have to be, the bound alone decides.
No kernel may reach another device: no remote copies, remote signals or barrier semaphores. Data moves between devices by JAX's collectives and lax.ppermute only.
A program may use at most 64 MiB of HBM per device.

v0:
```python
import jax
import jax.numpy as jnp
from jax import lax
from jax.sharding import PartitionSpec as P


def body(field, factor):
    rows_local, cells_local, cols_local = field.shape
    highest = lax.Precision.HIGHEST
    flat = field.reshape(rows_local, cells_local * cols_local)
    fibres = lax.all_to_all(flat, "aa", split_axis=1, concat_axis=0, tiled=True)
    partial_value = jnp.dot(fibres, fibres.T, precision=highest, preferred_element_type=jnp.float32)
    total = lax.psum(partial_value, ("aa", "ba", "col"))
    start = lax.axis_index("aa") * rows_local
    gram = lax.dynamic_slice_in_dim(total, start, rows_local, 0)
    whole_factor = lax.all_gather(factor, "aa", axis=0, tiled=True)
    columns = jnp.dot(whole_factor.T, fibres, precision=highest, preferred_element_type=jnp.float32)
    back = lax.all_to_all(columns, "aa", split_axis=0, concat_axis=1, tiled=True)
    truncated = back.reshape(back.shape[0], cells_local, cols_local)
    return (gram, truncated)


def solution(mesh):
    placed = (P("aa", "ba", "col"), P("aa", None))
    return jax.shard_map(
        body,
        mesh=mesh,
        in_specs=placed,
        out_specs=(P("aa", None), P("aa", "ba", "col")),
        check_vma=False,
    )
```

profile of v0, /device:TPU:1, one launch (start us, length us, event | category | flops | bytes accessed | tf_op | source)
XLA Modules:
  0.0 675.2 jit_solution(4311250255030219112)
XLA Ops:
  7.2 1.9 all_to_all.24
  9.1 2.6 copy.6
  11.7 0.0 copy-start
  11.7 18.5 %all-to-all-start = ((f32[32,16,1024]{2,0,1:T(8,128)}), f32[32,16,1024]{2,0,1:T(8,128)S(1)}, u32[]{:S(2)}, u32[]{:S(2)}) async-start(f32[32,16,1024]{2,0,1:T(8,128)} %copy.6), calls=%async_computation | async-start | bytes 4194304 | tf_op jit(solution)/shard_map/all_to_all | solution.py:11
  30.2 0.0 copy-done
  30.2 141.6 %all_gather.3 = f32[512,256]{1,0:T(8,128)S(1)} all-gather(f32[32,256]{1,0:T(8,128)S(1)} %copy-done), channel_id=1, replica_groups=mesh['aa'=16,'ba'=4,'col'=8] {'aa'}, dimensions={0}, use_global_device_ids=true | all-gather | bytes 557056 | tf_op jit(solution)/shard_map/all_gather | solution.py:16
  171.8 0.2 copy.7
  172.0 0.0 all-to-all-done
  172.0 2.9 fusion.1
  174.9 5.1 all-to-all-start.1
  180.0 0.0 all-reduce.2.cloned.1.call-start
  180.1 4.5 fusion
  184.6 0.0 all-reduce.2.cloned.1.call-update
  184.6 480.6 %all-reduce.2.cloned.1.call-done = f32[512,512]{1,0:T(8,128)} async-done(((f32[512,512]{1,0:T(8,128)}), f32[512,512]{1,0:T(8,128)}) %all-reduce.2.cloned.1.call-update) | async-done | bytes 1048592 | tf_op jit(solution)/shard_map/psum | solution.py:13
  665.1 1.5 constant_dynamic-slice_fusion
  666.6 0.0 all-to-all-done.1
  666.6 0.6 copy.8
  667.2 1.1 reshape.17
Async XLA Ops:
  11.7 18.5 %copy-start = (f32[32,256]{1,0:T(8,128)S(1)}, f32[32,256]{1,0:T(8,128)}, u32[]{:S(2)}) copy-start(f32[32,256]{1,0:T(8,128)} %param.3) | copy-start | bytes 98308
  11.7 160.4 %all-to-all-start = ((f32[32,16,1024]{2,0,1:T(8,128)}), f32[32,16,1024]{2,0,1:T(8,128)S(1)}, u32[]{:S(2)}, u32[]{:S(2)}) async-start(f32[32,16,1024]{2,0,1:T(8,128)} %copy.6), calls=%async_computation | async-start | bytes 4194304 | tf_op jit(solution)/shard_map/all_to_all | solution.py:11
  174.9 491.7 %all-to-all-start.1 = ((f32[16,16,1024]{2,1,0:T(8,128)}), f32[16,16,1024]{2,1,0:T(8,128)S(1)}, u32[]{:S(2)}, u32[]{:S(2)}) async-start(f32[16,16,1024]{2,1,0:T(8,128)} %fusion.1), calls=%async_computation.1 | async-start | bytes 2097152 | tf_op jit(solution)/shard_map/all_to_all | solution.py:18
  180.0 485.1 %all-reduce.2.cloned.1.call-start = ((), (), s32[]{:S(2)}) async-start(), calls=%async_computation.2 | async-start | bytes 2097152 | tf_op jit(solution)/shard_map/psum | solution.py:13
Sparse Core Ops, SparseCore 0:
  186.9 478.2 all-reduce.1
where the time goes:
time: 676 us; the launch traced here: 675 us
  waiting for transfers between devices  481 us (71%)
  blocking collectives  142 us (21%)
  starting transfers between devices  23.6 us (3%)
  between operations  14.1 us (2%)
  local copies, waits for them, and re-layouts  7.9 us (1%)
  matrix products  7.37 us (1%)
    psum x1, waiting for transfers between devices, body(): total = lax.psum(partial_value, ('aa', 'ba', 'col'))  481 us
    all_gather x1, blocking collectives, body(): whole_factor = lax.all_gather(factor, 'aa', axis=0, tiled=True)  142 us
    all_to_all x1, starting transfers between devices, body(): fibres = lax.all_to_all(flat, 'aa', split_axis=1, concat_axis=0, tiled=True)  18.5 us
  transfers between devices with their start and end apart: 3, of which 1 were waited for; matrix products, arithmetic and copies ran while one was open for 1% of the time, Pallas kernels for 0%

commit v1 on v0

v1 whole, which is shorter than its diff:
```python
import jax
import jax.numpy as jnp
from jax import lax
from jax.sharding import Mesh, PartitionSpec as P

AXES = ("zh", "y", "x", "zl", "core")
FIBRE = ("zh", "y")
PRECISION = lax.Precision.HIGH


def exchange(value, axis):
    return lax.all_to_all(value, axis, split_axis=0, concat_axis=0, tiled=True)


def swap(value, axis, flip):
    count = 2 if axis == "core" else 4
    return lax.ppermute(value, axis, [(i, i ^ flip) for i in range(count)])


def pick(value, index):
    return lax.dynamic_index_in_dim(value, index, 0, keepdims=False)


def scatter_sum(value, axis):
    own = lax.axis_index(axis)
    came = swap(jnp.stack([pick(value, own ^ 1), pick(value, own ^ 2)]), axis, 1)
    across = pick(value, own ^ 3) + came[1]
    return pick(value, own) + came[0] + swap(across, axis, 3)


def gather(value, axis):
    own = lax.axis_index(axis)
    pair = jnp.stack([value, swap(value, axis, 1)])
    far = swap(pair, axis, 3)
    by_flip = jnp.concatenate([pair, far[::-1]])
    return jnp.stack([pick(by_flip, own ^ j) for j in range(4)])


def gather_factor(factor):
    rows, kept = factor.shape
    part = lax.dynamic_slice_in_dim(factor, lax.axis_index("x") * (rows // 4), rows // 4, 0)
    return gather(part, "zh")


def spread_factor(parts):
    parts = gather(gather(parts, "y"), "x")
    return parts.transpose(2, 1, 0, 3, 4).reshape(-1, parts.shape[-1])


def reduce_gram(partial_gram):
    order = partial_gram.shape[0]
    half = order // 2
    core = lax.axis_index("core")
    other = lax.dynamic_slice_in_dim(partial_gram, (1 - core) * half, half, 1)
    own = lax.dynamic_slice_in_dim(partial_gram, core * half, half, 1)
    terms = (own + swap(other, "core", 1)).reshape(4, 4, order // 16, half)
    terms = scatter_sum(terms.transpose(1, 0, 2, 3), "y")
    rows = scatter_sum(terms, "zh")
    rows = rows + swap(rows, "zl", 1)
    rows = rows + swap(rows, "zl", 2)
    rows = rows + swap(rows, "x", 1)
    rows = rows + swap(rows, "x", 3)
    beside = swap(rows, "core", 1)
    return jnp.concatenate([jnp.where(core == 0, rows, beside), jnp.where(core == 0, beside, rows)], axis=1)


def body(field, factor):
    rows, cells, columns = field.shape
    blocks = field.reshape(rows, 16, cells * columns // 16).transpose(1, 0, 2)
    blocks, parts = lax.optimization_barrier((blocks, gather_factor(factor)))
    fibres = exchange(blocks, FIBRE).reshape(rows * 16, -1)
    whole_factor = spread_factor(parts)
    partial_gram = jnp.dot(fibres, fibres.T, precision=PRECISION, preferred_element_type=jnp.float32)
    cut = jnp.dot(whole_factor.T, fibres, precision=PRECISION, preferred_element_type=jnp.float32)
    back = exchange(cut.reshape(16, cut.shape[0] // 16, -1), FIBRE)
    gram = reduce_gram(partial_gram)
    truncated = back.transpose(1, 0, 2).reshape(back.shape[1], cells, columns)
    return gram, truncated


def solution(mesh):
    fine = Mesh(mesh.devices.reshape(4, 4, 4, 4, 2), AXES)
    last = ("zl", "core")
    return jax.shard_map(
        body,
        mesh=fine,
        in_specs=(P(FIBRE, "x", last), P(FIBRE, None)),
        out_specs=(P(FIBRE, None), P(FIBRE, "x", last)),
        check_vma=False,
    )
```

time: 676 us -> 241 us (0.36)
  waiting for transfers between devices: 481 us -> 113 us
  blocking collectives: 142 us -> 0 us
  starting transfers between devices: 23.6 us -> 112 us
  between operations: 14.1 us -> 1.03 us
    psum x1 -> x0, waiting for transfers between devices: 481 us -> none  [body(): total = lax.psum(partial_value, ('aa', 'ba', 'col'))]
    all_gather x1 -> x0, blocking collectives: 142 us -> none  [body(): whole_factor = lax.all_gather(factor, 'aa', axis=0, tiled=True)]
    ppermute x0 -> x16, starting transfers between devices: none -> 91.8 us  [swap(): return lax.ppermute(value, axis, [(i, i ^ flip) for i in range(count)])]
    all_to_all x2, waiting for transfers between devices: 0.01 us -> 66.6 us  [exchange(): return lax.all_to_all(value, axis, split_axis=0, concat_axis=0, tiled=True)]
    ppermute x0 -> x16, waiting for transfers between devices: none -> 46.2 us  [swap(): return lax.ppermute(value, axis, [(i, i ^ flip) for i in range(count)])]
  transfers between devices with their start and end apart: 3 -> 18, of which waited for: 1 -> 16; matrix products, arithmetic and copies ran while one was open for 1% -> 3% of each run, Pallas kernels for 0% -> 0%
where the time goes in v1:
time: 241 us; the launch traced here: 240 us
  waiting for transfers between devices  113 us (47%)
  starting transfers between devices  112 us (46%)
  local copies, waits for them, and re-layouts  8.6 us (4%)
  matrix products  3.9 us (2%)
    ppermute x16, starting transfers between devices, swap(): return lax.ppermute(value, axis, [(i, i ^ flip) for i in range(count)])  91.8 us
    all_to_all x2, waiting for transfers between devices, exchange(): return lax.all_to_all(value, axis, split_axis=0, concat_axis=0, tiled=True)  66.6 us
    ppermute x16, waiting for transfers between devices, swap(): return lax.ppermute(value, axis, [(i, i ^ flip) for i in range(count)])  46.2 us
    all_to_all x2, starting transfers between devices, exchange(): return lax.all_to_all(value, axis, split_axis=0, concat_axis=0, tiled=True)  20.6 us
  transfers between devices with their start and end apart: 18, of which 16 were waited for; matrix products, arithmetic and copies ran while one was open for 3% of the time, Pallas kernels for 0%

profile of v1, /device:TPU:1, one launch (start us, length us, event | category | flops | bytes accessed | tf_op | source)
XLA Modules:
  0.0 239.7 jit_solution(3694594180868912086)
XLA Ops:
  0.6 0.0 copy-start
  0.7 0.7 copy-done
  1.4 9.6 %collective-permute-start = (f32[8,256]{1,0:T(8,128)S(1)}, f32[8,256]{1,0:T(8,128)S(1)}, u32[]{:S(2)}, u32[]{:S(2)}) collective-permute-start(f32[8,256]{1,0:T(8,128)S(1)} %constant_dynamic-slice_fusion.15), channel_id=1, source_target_pairs={{0,128},{128,0},{256,384},{384,256},{1,129},{129,1},{257,385},{385... | collective-permute-start | bytes 24584 | tf_op jit(solution)/shard_map/ppermute | solution.py:17
  11.1 1.0 collective-permute-done
  12.1 10.9 %collective-permute-start.1 = (f32[2,8,256]{2,1,0:T(8,128)S(1)}, f32[2,8,256]{2,1,0:T(8,128)S(1)}, u32[]{:S(2)}, u32[]{:S(2)}) collective-permute-start(f32[2,8,256]{2,1,0:T(8,128)S(1)} %pad_maximum_fusion.11), channel_id=1, source_target_pairs={{0,384},{128,256},{256,128},{384,0},{1,385},{129,257},{257,129},{3... | collective-permute-start | bytes 49160 | tf_op jit(solution)/shard_map/ppermute | solution.py:17
  23.0 1.9 reshape.29
  24.9 2.5 %copy.13 = f32[32,16,1024]{2,0,1:T(8,128)} copy(f32[32,16,1024]{2,1,0:T(8,128)S(1)} %reshape.29) | data formatting | bytes 4194304 | tf_op jit(solution)/shard_map/reshape | solution.py:69
  27.5 0.0 collective-permute-done.1
  27.5 9.0 %all-to-all-start = ((f32[16,32,1024]{2,1,0:T(8,128)}), f32[16,32,1024]{2,1,0:T(8,128)S(1)}, u32[]{:S(2)}, u32[]{:S(2)}) async-start(f32[16,32,1024]{2,1,0:T(8,128)} %bitcast.58), calls=%async_computation | async-start | bytes 4194304 | tf_op jit(solution)/shard_map/all_to_all | solution.py:12
  36.5 3.3 %collective-permute-start.12 = (f32[4,8,256]{2,1,0:T(8,128)S(1)}, f32[4,8,256]{2,1,0:T(8,128)S(1)}, u32[]{:S(2)}, u32[]{:S(2)}) collective-permute-start(f32[4,8,256]{2,1,0:T(8,128)S(1)} %pad_maximum_fusion.10), channel_id=1, source_target_pairs={{0,32},{32,0},{64,96},{96,64},{1,33},{33,1},{65,97},{97,65},{2,34}... | collective-permute-start | bytes 98312 | tf_op jit(solution)/shard_map/ppermute | solution.py:17
  39.8 2.4 %collective-permute-done.12 = f32[4,8,256]{2,1,0:T(8,128)S(1)} collective-permute-done((f32[4,8,256]{2,1,0:T(8,128)S(1)}, f32[4,8,256]{2,1,0:T(8,128)S(1)}, u32[]{:S(2)}, u32[]{:S(2)}) %collective-permute-start.12) | collective-permute-done | bytes 32800 | tf_op jit(solution)/shard_map/ppermute | solution.py:17
  42.2 4.0 %collective-permute-start.13 = (f32[2,4,8,256]{3,2,0,1:T(8,128)S(1)}, f32[2,4,8,256]{3,2,0,1:T(8,128)S(1)}, u32[]{:S(2)}, u32[]{:S(2)}) collective-permute-start(f32[2,4,8,256]{3,2,0,1:T(8,128)S(1)} %pad_maximum_fusion.8), channel_id=1, source_target_pairs={{0,96},{32,64},{64,32},{96,0},{1,97},{33,65},{65,33},{97,1},{2,98}... | collective-permute-start | bytes 196616 | tf_op jit(solution)/shard_map/ppermute | solution.py:17
  46.2 2.5 %collective-permute-done.13 = f32[2,4,8,256]{3,2,0,1:T(8,128)S(1)} collective-permute-done((f32[2,4,8,256]{3,2,0,1:T(8,128)S(1)}, f32[2,4,8,256]{3,2,0,1:T(8,128)S(1)}, u32[]{:S(2)}, u32[]{:S(2)}) %collective-permute-start.13) | collective-permute-done | bytes 65568 | tf_op jit(solution)/shard_map/ppermute | solution.py:17
  48.8 3.1 %collective-permute-start.14 = (f32[4,4,8,256]{3,2,0,1:T(8,128)S(1)}, f32[4,4,8,256]{3,2,0,1:T(8,128)S(1)}, u32[]{:S(2)}, u32[]{:S(2)}) collective-permute-start(f32[4,4,8,256]{3,2,0,1:T(8,128)S(1)} %get-tuple-element.13), channel_id=1, source_target_pairs={{0,8},{8,0},{16,24},{24,16},{1,9},{9,1},{17,25},{25,17},{2,10},{10... | collective-permute-start | bytes 393224 | tf_op jit(solution)/shard_map/ppermute | solution.py:17
  51.9 2.9 %collective-permute-done.14 = f32[4,4,8,256]{3,2,0,1:T(8,128)S(1)} collective-permute-done((f32[4,4,8,256]{3,2,0,1:T(8,128)S(1)}, f32[4,4,8,256]{3,2,0,1:T(8,128)S(1)}, u32[]{:S(2)}, u32[]{:S(2)}) %collective-permute-start.14) | collective-permute-done | bytes 131104 | tf_op jit(solution)/shard_map/ppermute | solution.py:17
  54.8 4.4 %collective-permute-start.15 = (f32[2,4,4,8,256]{4,3,0,1,2:T(8,128)S(1)}, f32[2,4,4,8,256]{4,3,0,1,2:T(8,128)S(1)}, u32[]{:S(2)}, u32[]{:S(2)}) collective-permute-start(f32[2,4,4,8,256]{4,3,0,1,2:T(8,128)S(1)} %pad_maximum_fusion.3), channel_id=1, source_target_pairs={{0,24},{8,16},{16,8},{24,0},{1,25},{9,17},{17,9},{25,1},{2,26},{10... | collective-permute-start | bytes 786440 | tf_op jit(solution)/shard_map/ppermute | solution.py:17
  59.2 4.2 %collective-permute-done.15 = f32[2,4,4,8,256]{4,3,0,1,2:T(8,128)S(1)} collective-permute-done((f32[2,4,4,8,256]{4,3,0,1,2:T(8,128)S(1)}, f32[2,4,4,8,256]{4,3,0,1,2:T(8,128)S(1)}, u32[]{:S(2)}, u32[]{:S(2)}) %collective-permute-start.15) | collective-permute-done | bytes 262176 | tf_op jit(solution)/shard_map/ppermute | solution.py:17
  63.6 0.2 copy.10
  63.8 66.6 %all-to-all-done = f32[16,32,1024]{2,1,0:T(8,128)S(1)} async-done(((f32[16,32,1024]{2,1,0:T(8,128)}), f32[16,32,1024]{2,1,0:T(8,128)S(1)}, u32[]{:S(2)}, u32[]{:S(2)}) %all-to-all-start) | async-done | bytes 2097184 | tf_op jit(solution)/shard_map/all_to_all | solution.py:12
  130.4 2.1 fusion.8
  132.4 11.7 %all-to-all-start.1 = ((f32[16,16,1024]{2,1,0:T(8,128)}), f32[16,16,1024]{2,1,0:T(8,128)}, u32[]{:S(2)}, u32[]{:S(2)}) async-start(f32[16,16,1024]{2,1,0:T(8,128)} %fusion.8), calls=%async_computation.1 | async-start | bytes 2097152 | tf_op jit(solution)/shard_map/all_to_all | solution.py:12
  144.1 1.8 fusion.7
  146.0 3.2 %collective-permute-start.2 = (f32[512,256]{1,0:T(8,128)S(1)}, f32[512,256]{1,0:T(8,128)S(1)}, u32[]{:S(2)}, u32[]{:S(2)}) collective-permute-start(f32[512,256]{1,0:T(8,128)S(1)} %constant_dynamic-slice_fusion.10), channel_id=1, source_target_pairs={{0,1},{1,0},{2,3},{3,2},{4,5},{5,4},{6,7},{7,6},{8,9},{9,8},{10,11... | collective-permute-start | bytes 1572872 | tf_op jit(solution)/shard_map/ppermute | solution.py:17
  149.3 1.5 collective-permute-done.2
  150.8 0.1 dynamic-slice_add_fusion
  151.0 3.5 %collective-permute-start.3 = (f32[2,4,32,256]{3,2,1,0:T(8,128)S(1)}, f32[2,4,32,256]{3,2,1,0:T(8,128)S(1)}, u32[]{:S(2)}, u32[]{:S(2)}) collective-permute-start(f32[2,4,32,256]{3,2,1,0:T(8,128)S(1)} %pad_maximum_fusion.2), channel_id=1, source_target_pairs={{0,32},{32,0},{64,96},{96,64},{1,33},{33,1},{65,97},{97,65},{2,34}... | collective-permute-start | bytes 786440 | tf_op jit(solution)/shard_map/ppermute | solution.py:17
  154.5 6.5 %collective-permute-done.3 = f32[2,4,32,256]{3,2,1,0:T(8,128)S(1)} collective-permute-done((f32[2,4,32,256]{3,2,1,0:T(8,128)S(1)}, f32[2,4,32,256]{3,2,1,0:T(8,128)S(1)}, u32[]{:S(2)}, u32[]{:S(2)}) %collective-permute-start.3) | collective-permute-done | bytes 262176 | tf_op jit(solution)/shard_map/ppermute | solution.py:17
  161.0 4.7 %collective-permute-start.4 = (f32[4,32,256]{2,1,0:T(8,128)S(1)}, f32[4,32,256]{2,1,0:T(8,128)S(1)}, u32[]{:S(2)}, u32[]{:S(2)}) collective-permute-start(f32[4,32,256]{2,1,0:T(8,128)S(1)} %fusion), channel_id=1, source_target_pairs={{0,96},{32,64},{64,32},{96,0},{1,97},{33,65},{65,33},{97,1},{2,98}... | collective-permute-start | bytes 393224 | tf_op jit(solution)/shard_map/ppermute | solution.py:17
  165.8 2.8 %collective-permute-done.4 = f32[4,32,256]{2,1,0:T(8,128)S(1)} collective-permute-done((f32[4,32,256]{2,1,0:T(8,128)S(1)}, f32[4,32,256]{2,1,0:T(8,128)S(1)}, u32[]{:S(2)}, u32[]{:S(2)}) %collective-permute-start.4) | collective-permute-done | bytes 131104 | tf_op jit(solution)/shard_map/ppermute | solution.py:17
  168.6 6.9 %collective-permute-start.5 = (f32[2,32,256]{2,1,0:T(8,128)S(1)}, f32[2,32,256]{2,1,0:T(8,128)S(1)}, u32[]{:S(2)}, u32[]{:S(2)}) collective-permute-start(f32[2,32,256]{2,1,0:T(8,128)S(1)} %pad_maximum_fusion.6), channel_id=1, source_target_pairs={{0,128},{128,0},{256,384},{384,256},{1,129},{129,1},{257,385},{385... | collective-permute-start | bytes 196616 | tf_op jit(solution)/shard_map/ppermute | solution.py:17
  175.5 11.3 %collective-permute-done.5 = f32[2,32,256]{2,1,0:T(8,128)S(1)} collective-permute-done((f32[2,32,256]{2,1,0:T(8,128)S(1)}, f32[2,32,256]{2,1,0:T(8,128)S(1)}, u32[]{:S(2)}, u32[]{:S(2)}) %collective-permute-start.5) | collective-permute-done | bytes 65568 | tf_op jit(solution)/shard_map/ppermute | solution.py:17
  186.8 12.0 %collective-permute-start.6 = (f32[32,256]{1,0:T(8,128)S(1)}, f32[32,256]{1,0:T(8,128)S(1)}, u32[]{:S(2)}, u32[]{:S(2)}) collective-permute-start(f32[32,256]{1,0:T(8,128)S(1)} %fusion.3), channel_id=1, source_target_pairs={{0,384},{128,256},{256,128},{384,0},{1,385},{129,257},{257,129},{3... | collective-permute-start | bytes 98312 | tf_op jit(solution)/shard_map/ppermute | solution.py:17
  198.9 4.3 %collective-permute-done.6 = f32[32,256]{1,0:T(8,128)S(1)} collective-permute-done((f32[32,256]{1,0:T(8,128)S(1)}, f32[32,256]{1,0:T(8,128)S(1)}, u32[]{:S(2)}, u32[]{:S(2)}) %collective-permute-start.6) | collective-permute-done | bytes 32800 | tf_op jit(solution)/shard_map/ppermute | solution.py:17
  203.2 3.4 %collective-permute-start.7 = (f32[32,256]{1,0:T(8,128)S(1)}, f32[32,256]{1,0:T(8,128)S(1)}, u32[]{:S(2)}, u32[]{:S(2)}) collective-permute-start(f32[32,256]{1,0:T(8,128)S(1)} %fusion.5), channel_id=1, source_target_pairs={{0,2},{2,0},{4,6},{6,4},{1,3},{3,1},{5,7},{7,5},{8,10},{10,8},{12,... | collective-permute-start | bytes 98312 | tf_op jit(solution)/shard_map/ppermute | solution.py:17
  206.6 1.6 collective-permute-done.7
  208.3 6.5 %collective-permute-start.8 = (f32[32,256]{1,0:T(8,128)S(1)}, f32[32,256]{1,0:T(8,128)S(1)}, u32[]{:S(2)}, u32[]{:S(2)}) collective-permute-start(f32[32,256]{1,0:T(8,128)S(1)} %add.117), channel_id=1, source_target_pairs={{0,4},{2,6},{4,0},{6,2},{1,5},{3,7},{5,1},{7,3},{8,12},{10,14},{12... | collective-permute-start | bytes 98312 | tf_op jit(solution)/shard_map/ppermute | solution.py:17
  214.8 1.3 collective-permute-done.8
  216.1 3.1 %collective-permute-start.9 = (f32[32,256]{1,0:T(8,128)S(1)}, f32[32,256]{1,0:T(8,128)S(1)}, u32[]{:S(2)}, u32[]{:S(2)}) collective-permute-start(f32[32,256]{1,0:T(8,128)S(1)} %add.118), channel_id=1, source_target_pairs={{0,8},{8,0},{16,24},{24,16},{1,9},{9,1},{17,25},{25,17},{2,10},{10... | collective-permute-start | bytes 98312 | tf_op jit(solution)/shard_map/ppermute | solution.py:17
  219.2 1.5 collective-permute-done.9
  220.7 4.3 %collective-permute-start.10 = (f32[32,256]{1,0:T(8,128)S(1)}, f32[32,256]{1,0:T(8,128)S(1)}, u32[]{:S(2)}, u32[]{:S(2)}) collective-permute-start(f32[32,256]{1,0:T(8,128)S(1)} %add.119), channel_id=1, source_target_pairs={{0,24},{8,16},{16,8},{24,0},{1,25},{9,17},{17,9},{25,1},{2,26},{10... | collective-permute-start | bytes 98312 | tf_op jit(solution)/shard_map/ppermute | solution.py:17
  225.1 1.5 collective-permute-done.10
  226.6 8.7 %collective-permute-start.11 = (f32[32,256]{1,0:T(8,128)S(1)}, f32[32,256]{1,0:T(8,128)S(1)}, u32[]{:S(2)}, u32[]{:S(2)}) collective-permute-start(f32[32,256]{1,0:T(8,128)S(1)} %add.120), channel_id=1, source_target_pairs={{0,1},{1,0},{2,3},{3,2},{4,5},{5,4},{6,7},{7,6},{8,9},{9,8},{10,11... | collective-permute-start | bytes 98312 | tf_op jit(solution)/shard_map/ppermute | solution.py:17
  235.3 0.8 collective-permute-done.11
  236.1 0.6 pad_maximum_fusion.7
  236.8 0.0 all-to-all-done.1
  236.8 1.8 copy.11
  238.6 1.1 reshape.33
  (31 shorter events, 0.5 us)
Async XLA Ops:
  0.6 0.8 copy-start
  1.4 10.7 %collective-permute-start = (f32[8,256]{1,0:T(8,128)S(1)}, f32[8,256]{1,0:T(8,128)S(1)}, u32[]{:S(2)}, u32[]{:S(2)}) collective-permute-start(f32[8,256]{1,0:T(8,128)S(1)} %constant_dynamic-slice_fusion.15), channel_id=1, source_target_pairs={{0,128},{128,0},{256,384},{384,256},{1,129},{129,1},{257,385},{385... | collective-permute-start | bytes 24584 | tf_op jit(solution)/shard_map/ppermute | solution.py:17
  12.1 15.4 %collective-permute-start.1 = (f32[2,8,256]{2,1,0:T(8,128)S(1)}, f32[2,8,256]{2,1,0:T(8,128)S(1)}, u32[]{:S(2)}, u32[]{:S(2)}) collective-permute-start(f32[2,8,256]{2,1,0:T(8,128)S(1)} %pad_maximum_fusion.11), channel_id=1, source_target_pairs={{0,384},{128,256},{256,128},{384,0},{1,385},{129,257},{257,129},{3... | collective-permute-start | bytes 49160 | tf_op jit(solution)/shard_map/ppermute | solution.py:17
  27.5 102.9 %all-to-all-start = ((f32[16,32,1024]{2,1,0:T(8,128)}), f32[16,32,1024]{2,1,0:T(8,128)S(1)}, u32[]{:S(2)}, u32[]{:S(2)}) async-start(f32[16,32,1024]{2,1,0:T(8,128)} %bitcast.58), calls=%async_computation | async-start | bytes 4194304 | tf_op jit(solution)/shard_map/all_to_all | solution.py:12
  36.5 5.7 %collective-permute-start.12 = (f32[4,8,256]{2,1,0:T(8,128)S(1)}, f32[4,8,256]{2,1,0:T(8,128)S(1)}, u32[]{:S(2)}, u32[]{:S(2)}) collective-permute-start(f32[4,8,256]{2,1,0:T(8,128)S(1)} %pad_maximum_fusion.10), channel_id=1, source_target_pairs={{0,32},{32,0},{64,96},{96,64},{1,33},{33,1},{65,97},{97,65},{2,34}... | collective-permute-start | bytes 98312 | tf_op jit(solution)/shard_map/ppermute | solution.py:17
  42.2 6.5 %collective-permute-start.13 = (f32[2,4,8,256]{3,2,0,1:T(8,128)S(1)}, f32[2,4,8,256]{3,2,0,1:T(8,128)S(1)}, u32[]{:S(2)}, u32[]{:S(2)}) collective-permute-start(f32[2,4,8,256]{3,2,0,1:T(8,128)S(1)} %pad_maximum_fusion.8), channel_id=1, source_target_pairs={{0,96},{32,64},{64,32},{96,0},{1,97},{33,65},{65,33},{97,1},{2,98}... | collective-permute-start | bytes 196616 | tf_op jit(solution)/shard_map/ppermute | solution.py:17
  48.8 6.0 %collective-permute-start.14 = (f32[4,4,8,256]{3,2,0,1:T(8,128)S(1)}, f32[4,4,8,256]{3,2,0,1:T(8,128)S(1)}, u32[]{:S(2)}, u32[]{:S(2)}) collective-permute-start(f32[4,4,8,256]{3,2,0,1:T(8,128)S(1)} %get-tuple-element.13), channel_id=1, source_target_pairs={{0,8},{8,0},{16,24},{24,16},{1,9},{9,1},{17,25},{25,17},{2,10},{10... | collective-permute-start | bytes 393224 | tf_op jit(solution)/shard_map/ppermute | solution.py:17
  54.8 8.6 %collective-permute-start.15 = (f32[2,4,4,8,256]{4,3,0,1,2:T(8,128)S(1)}, f32[2,4,4,8,256]{4,3,0,1,2:T(8,128)S(1)}, u32[]{:S(2)}, u32[]{:S(2)}) collective-permute-start(f32[2,4,4,8,256]{4,3,0,1,2:T(8,128)S(1)} %pad_maximum_fusion.3), channel_id=1, source_target_pairs={{0,24},{8,16},{16,8},{24,0},{1,25},{9,17},{17,9},{25,1},{2,26},{10... | collective-permute-start | bytes 786440 | tf_op jit(solution)/shard_map/ppermute | solution.py:17
  132.4 104.3 %all-to-all-start.1 = ((f32[16,16,1024]{2,1,0:T(8,128)}), f32[16,16,1024]{2,1,0:T(8,128)}, u32[]{:S(2)}, u32[]{:S(2)}) async-start(f32[16,16,1024]{2,1,0:T(8,128)} %fusion.8), calls=%async_computation.1 | async-start | bytes 2097152 | tf_op jit(solution)/shard_map/all_to_all | solution.py:12
  146.0 4.8 %collective-permute-start.2 = (f32[512,256]{1,0:T(8,128)S(1)}, f32[512,256]{1,0:T(8,128)S(1)}, u32[]{:S(2)}, u32[]{:S(2)}) collective-permute-start(f32[512,256]{1,0:T(8,128)S(1)} %constant_dynamic-slice_fusion.10), channel_id=1, source_target_pairs={{0,1},{1,0},{2,3},{3,2},{4,5},{5,4},{6,7},{7,6},{8,9},{9,8},{10,11... | collective-permute-start | bytes 1572872 | tf_op jit(solution)/shard_map/ppermute | solution.py:17
  151.0 10.0 %collective-permute-start.3 = (f32[2,4,32,256]{3,2,1,0:T(8,128)S(1)}, f32[2,4,32,256]{3,2,1,0:T(8,128)S(1)}, u32[]{:S(2)}, u32[]{:S(2)}) collective-permute-start(f32[2,4,32,256]{3,2,1,0:T(8,128)S(1)} %pad_maximum_fusion.2), channel_id=1, source_target_pairs={{0,32},{32,0},{64,96},{96,64},{1,33},{33,1},{65,97},{97,65},{2,34}... | collective-permute-start | bytes 786440 | tf_op jit(solution)/shard_map/ppermute | solution.py:17
  161.0 7.5 %collective-permute-start.4 = (f32[4,32,256]{2,1,0:T(8,128)S(1)}, f32[4,32,256]{2,1,0:T(8,128)S(1)}, u32[]{:S(2)}, u32[]{:S(2)}) collective-permute-start(f32[4,32,256]{2,1,0:T(8,128)S(1)} %fusion), channel_id=1, source_target_pairs={{0,96},{32,64},{64,32},{96,0},{1,97},{33,65},{65,33},{97,1},{2,98}... | collective-permute-start | bytes 393224 | tf_op jit(solution)/shard_map/ppermute | solution.py:17
  168.6 18.2 %collective-permute-start.5 = (f32[2,32,256]{2,1,0:T(8,128)S(1)}, f32[2,32,256]{2,1,0:T(8,128)S(1)}, u32[]{:S(2)}, u32[]{:S(2)}) collective-permute-start(f32[2,32,256]{2,1,0:T(8,128)S(1)} %pad_maximum_fusion.6), channel_id=1, source_target_pairs={{0,128},{128,0},{256,384},{384,256},{1,129},{129,1},{257,385},{385... | collective-permute-start | bytes 196616 | tf_op jit(solution)/shard_map/ppermute | solution.py:17
  186.8 16.3 %collective-permute-start.6 = (f32[32,256]{1,0:T(8,128)S(1)}, f32[32,256]{1,0:T(8,128)S(1)}, u32[]{:S(2)}, u32[]{:S(2)}) collective-permute-start(f32[32,256]{1,0:T(8,128)S(1)} %fusion.3), channel_id=1, source_target_pairs={{0,384},{128,256},{256,128},{384,0},{1,385},{129,257},{257,129},{3... | collective-permute-start | bytes 98312 | tf_op jit(solution)/shard_map/ppermute | solution.py:17
  203.2 5.1 %collective-permute-start.7 = (f32[32,256]{1,0:T(8,128)S(1)}, f32[32,256]{1,0:T(8,128)S(1)}, u32[]{:S(2)}, u32[]{:S(2)}) collective-permute-start(f32[32,256]{1,0:T(8,128)S(1)} %fusion.5), channel_id=1, source_target_pairs={{0,2},{2,0},{4,6},{6,4},{1,3},{3,1},{5,7},{7,5},{8,10},{10,8},{12,... | collective-permute-start | bytes 98312 | tf_op jit(solution)/shard_map/ppermute | solution.py:17
  208.3 7.8 %collective-permute-start.8 = (f32[32,256]{1,0:T(8,128)S(1)}, f32[32,256]{1,0:T(8,128)S(1)}, u32[]{:S(2)}, u32[]{:S(2)}) collective-permute-start(f32[32,256]{1,0:T(8,128)S(1)} %add.117), channel_id=1, source_target_pairs={{0,4},{2,6},{4,0},{6,2},{1,5},{3,7},{5,1},{7,3},{8,12},{10,14},{12... | collective-permute-start | bytes 98312 | tf_op jit(solution)/shard_map/ppermute | solution.py:17
  216.1 4.6 %collective-permute-start.9 = (f32[32,256]{1,0:T(8,128)S(1)}, f32[32,256]{1,0:T(8,128)S(1)}, u32[]{:S(2)}, u32[]{:S(2)}) collective-permute-start(f32[32,256]{1,0:T(8,128)S(1)} %add.118), channel_id=1, source_target_pairs={{0,8},{8,0},{16,24},{24,16},{1,9},{9,1},{17,25},{25,17},{2,10},{10... | collective-permute-start | bytes 98312 | tf_op jit(solution)/shard_map/ppermute | solution.py:17
  220.7 5.9 %collective-permute-start.10 = (f32[32,256]{1,0:T(8,128)S(1)}, f32[32,256]{1,0:T(8,128)S(1)}, u32[]{:S(2)}, u32[]{:S(2)}) collective-permute-start(f32[32,256]{1,0:T(8,128)S(1)} %add.119), channel_id=1, source_target_pairs={{0,24},{8,16},{16,8},{24,0},{1,25},{9,17},{17,9},{25,1},{2,26},{10... | collective-permute-start | bytes 98312 | tf_op jit(solution)/shard_map/ppermute | solution.py:17
  226.6 9.5 %collective-permute-start.11 = (f32[32,256]{1,0:T(8,128)S(1)}, f32[32,256]{1,0:T(8,128)S(1)}, u32[]{:S(2)}, u32[]{:S(2)}) collective-permute-start(f32[32,256]{1,0:T(8,128)S(1)} %add.120), channel_id=1, source_target_pairs={{0,1},{1,0},{2,3},{3,2},{4,5},{5,4},{6,7},{7,6},{8,9},{9,8},{10,11... | collective-permute-start | bytes 98312 | tf_op jit(solution)/shard_map/ppermute | solution.py:17

commit v2 on v1

v2 whole, which is shorter than its diff:
```python
import jax
import jax.numpy as jnp
from jax import lax
from jax.sharding import Mesh, PartitionSpec as P

AXES = ("zh", "y", "x", "zl", "core")
FIBRE = ("zh", "y")
PRECISION = lax.Precision.HIGH
F32 = jnp.float32


def exchange(value, axis):
    return lax.all_to_all(value, axis, split_axis=0, concat_axis=0, tiled=True)


def swap(value, axis, flip):
    count = 2 if axis == "core" else 4
    return lax.ppermute(value, axis, [(i, i ^ flip) for i in range(count)])


def pick(value, index):
    return lax.dynamic_index_in_dim(value, index, 0, keepdims=False)


def by_owner(by_flip, own):
    held = jnp.stack(by_flip)
    return jnp.stack([pick(held, own ^ j) for j in range(4)])


def sum_swapped(parts, axis):
    far = [swap(parts[k], axis, k) for k in (2, 1, 3)]
    return (parts[0] + far[1]) + (far[0] + far[2])


def scatter_sum(value, axis):
    own = lax.axis_index(axis)
    return sum_swapped([pick(value, own ^ k) for k in range(4)], axis)


def gather(value, axis):
    own = lax.axis_index(axis)
    pair = jnp.stack([value, swap(value, axis, 1)])
    far = swap(pair, axis, 3)
    return by_owner([pair[0], pair[1], far[1], far[0]], own)


def gather_zh(factor):
    rows = factor.shape[0] // 4
    part = lax.dynamic_slice_in_dim(factor, lax.axis_index("x") * rows, rows, 0)
    return [part] + [swap(part, "zh", k) for k in (1, 2, 3)]


def spread_factor(parts):
    parts = gather(gather(by_owner(parts, lax.axis_index("zh")), "y"), "x")
    return parts.transpose(2, 1, 0, 3, 4).reshape(-1, parts.shape[-1])


def reduce_gram(partial_gram):
    order = partial_gram.shape[0]
    half = order // 2
    core = lax.axis_index("core")
    other = lax.dynamic_slice_in_dim(partial_gram, (1 - core) * half, half, 1)
    own = lax.dynamic_slice_in_dim(partial_gram, core * half, half, 1)
    terms = (own + swap(other, "core", 1)).reshape(4, 4, order // 16, half)
    terms = scatter_sum(terms.transpose(1, 0, 2, 3), "y")
    terms = sum_swapped([terms] * 4, "x")
    rows = scatter_sum(terms, "zh")
    rows = rows + swap(rows, "zl", 1)
    rows = rows + swap(rows, "zl", 2)
    beside = swap(rows, "core", 1)
    return jnp.concatenate([jnp.where(core == 0, rows, beside), jnp.where(core == 0, beside, rows)], axis=1)


def dot(a, b):
    return jnp.dot(a, b, precision=PRECISION, preferred_element_type=F32)


def body(field, factor):
    rows, cells, columns = field.shape
    blocks = field.reshape(rows, 16, cells * columns // 16).transpose(1, 0, 2)
    blocks, parts = lax.optimization_barrier((blocks, gather_zh(factor)))
    fibres = exchange(blocks, FIBRE).reshape(rows * 16, -1)
    whole_factor = spread_factor(parts)
    cut = dot(whole_factor.T, fibres)
    kept = cut.shape[0] // 16
    back = exchange(cut.reshape(16, kept, -1), FIBRE)
    gram = reduce_gram(dot(fibres, fibres.T))
    return gram, back.transpose(1, 0, 2).reshape(kept, cells, columns)


def solution(mesh):
    fine = Mesh(mesh.devices.reshape(4, 4, 4, 4, 2), AXES)
    last = ("zl", "core")
    return jax.shard_map(
        body,
        mesh=fine,
        in_specs=(P(FIBRE, "x", last), P(FIBRE, None)),
        out_specs=(P(FIBRE, None), P(FIBRE, "x", last)),
        check_vma=False,
    )
```

time: 241 us -> 232 us (0.963)
  waiting for transfers between devices: 113 us -> 104 us
    ppermute x16 -> x20, waiting for transfers between devices: 46.2 us -> 39.1 us  [swap(): return lax.ppermute(value, axis, [(i, i ^ flip) for i in range(count)])]
    ppermute x16 -> x20, starting transfers between devices: 91.8 us -> 89.7 us  [swap(): return lax.ppermute(value, axis, [(i, i ^ flip) for i in range(count)])]
  transfers between devices with their start and end apart: 18 -> 22, of which waited for: 16 -> 17; matrix products, arithmetic and copies ran while one was open for 3% -> 3% of each run, Pallas kernels for 0% -> 0%
where the time goes in v2:
time: 232 us; the launch traced here: 231 us
  starting transfers between devices  113 us (49%)
  waiting for transfers between devices  104 us (45%)
  local copies, waits for them, and re-layouts  8.62 us (4%)
  matrix products  3.9 us (2%)
    ppermute x20, starting transfers between devices, swap(): return lax.ppermute(value, axis, [(i, i ^ flip) for i in range(count)])  89.7 us
    all_to_all x2, waiting for transfers between devices, exchange(): return lax.all_to_all(value, axis, split_axis=0, concat_axis=0, tiled=True)  64.7 us
    ppermute x20, waiting for transfers between devices, swap(): return lax.ppermute(value, axis, [(i, i ^ flip) for i in range(count)])  39.1 us
    all_to_all x2, starting transfers between devices, exchange(): return lax.all_to_all(value, axis, split_axis=0, concat_axis=0, tiled=True)  23 us
  transfers between devices with their start and end apart: 22, of which 17 were waited for; matrix products, arithmetic and copies ran while one was open for 3% of the time, Pallas kernels for 0%

profile of v2, /device:TPU:1, one launch (start us, length us, event | category | flops | bytes accessed | tf_op | source)
XLA Modules:
  0.0 231.1 jit_solution(11570799098122183797)
XLA Ops:
  0.6 0.0 copy-start
  0.7 0.7 copy-done
  1.4 9.6 %collective-permute-start = (f32[8,256]{1,0:T(8,128)S(1)}, f32[8,256]{1,0:T(8,128)S(1)}, u32[]{:S(2)}, u32[]{:S(2)}) collective-permute-start(f32[8,256]{1,0:T(8,128)S(1)} %constant_dynamic-slice_fusion.13), channel_id=1, source_target_pairs={{0,128},{128,0},{256,384},{384,256},{1,129},{129,1},{257,385},{385... | collective-permute-start | bytes 24584 | tf_op jit(solution)/shard_map/ppermute | solution.py:18
  11.0 10.6 %collective-permute-start.1 = (f32[8,256]{1,0:T(8,128)S(1)}, f32[8,256]{1,0:T(8,128)S(1)}, u32[]{:S(2)}, u32[]{:S(2)}) collective-permute-start(f32[8,256]{1,0:T(8,128)S(1)} %constant_dynamic-slice_fusion.13), channel_id=1, source_target_pairs={{0,256},{128,384},{256,0},{384,128},{1,257},{129,385},{257,1},{385... | collective-permute-start | bytes 24584 | tf_op jit(solution)/shard_map/ppermute | solution.py:18
  21.7 1.9 collective-permute-start.2
  23.6 1.9 reshape.29
  25.6 2.6 %copy.13 = f32[32,16,1024]{2,0,1:T(8,128)} copy(f32[32,16,1024]{2,1,0:T(8,128)S(1)} %reshape.29) | data formatting | bytes 4194304 | tf_op jit(solution)/shard_map/reshape | solution.py:80
  28.1 0.0 collective-permute-done
  28.1 0.0 collective-permute-done.1
  28.1 1.9 collective-permute-done.2
  30.0 10.5 %all-to-all-start = ((f32[16,32,1024]{2,1,0:T(8,128)}), f32[16,32,1024]{2,1,0:T(8,128)S(1)}, u32[]{:S(2)}, u32[]{:S(2)}) async-start(f32[16,32,1024]{2,1,0:T(8,128)} %bitcast.56), calls=%async_computation | async-start | bytes 4194304 | tf_op jit(solution)/shard_map/all_to_all | solution.py:13
  40.6 3.2 %collective-permute-start.16 = (f32[4,8,256]{2,1,0:T(8,128)S(1)}, f32[4,8,256]{2,1,0:T(8,128)S(1)}, u32[]{:S(2)}, u32[]{:S(2)}) collective-permute-start(f32[4,8,256]{2,1,0:T(8,128)S(1)} %get-tuple-element.35), channel_id=1, source_target_pairs={{0,32},{32,0},{64,96},{96,64},{1,33},{33,1},{65,97},{97,65},{2,34}... | collective-permute-start | bytes 98312 | tf_op jit(solution)/shard_map/ppermute | solution.py:18
  43.8 3.5 %collective-permute-done.16 = f32[4,8,256]{2,1,0:T(8,128)S(1)} collective-permute-done((f32[4,8,256]{2,1,0:T(8,128)S(1)}, f32[4,8,256]{2,1,0:T(8,128)S(1)}, u32[]{:S(2)}, u32[]{:S(2)}) %collective-permute-start.16) | collective-permute-done | bytes 32800 | tf_op jit(solution)/shard_map/ppermute | solution.py:18
  47.3 3.8 %collective-permute-start.17 = (f32[2,4,8,256]{3,2,0,1:T(8,128)S(1)}, f32[2,4,8,256]{3,2,0,1:T(8,128)S(1)}, u32[]{:S(2)}, u32[]{:S(2)}) collective-permute-start(f32[2,4,8,256]{3,2,0,1:T(8,128)S(1)} %pad_maximum_fusion.6), channel_id=1, source_target_pairs={{0,96},{32,64},{64,32},{96,0},{1,97},{33,65},{65,33},{97,1},{2,98}... | collective-permute-start | bytes 196616 | tf_op jit(solution)/shard_map/ppermute | solution.py:18
  51.1 2.7 %collective-permute-done.17 = f32[2,4,8,256]{3,2,0,1:T(8,128)S(1)} collective-permute-done((f32[2,4,8,256]{3,2,0,1:T(8,128)S(1)}, f32[2,4,8,256]{3,2,0,1:T(8,128)S(1)}, u32[]{:S(2)}, u32[]{:S(2)}) %collective-permute-start.17) | collective-permute-done | bytes 65568 | tf_op jit(solution)/shard_map/ppermute | solution.py:18
  53.9 3.1 %collective-permute-start.18 = (f32[4,4,8,256]{3,2,0,1:T(8,128)S(1)}, f32[4,4,8,256]{3,2,0,1:T(8,128)S(1)}, u32[]{:S(2)}, u32[]{:S(2)}) collective-permute-start(f32[4,4,8,256]{3,2,0,1:T(8,128)S(1)} %get-tuple-element.22), channel_id=1, source_target_pairs={{0,8},{8,0},{16,24},{24,16},{1,9},{9,1},{17,25},{25,17},{2,10},{10... | collective-permute-start | bytes 393224 | tf_op jit(solution)/shard_map/ppermute | solution.py:18
  57.0 2.9 %collective-permute-done.18 = f32[4,4,8,256]{3,2,0,1:T(8,128)S(1)} collective-permute-done((f32[4,4,8,256]{3,2,0,1:T(8,128)S(1)}, f32[4,4,8,256]{3,2,0,1:T(8,128)S(1)}, u32[]{:S(2)}, u32[]{:S(2)}) %collective-permute-start.18) | collective-permute-done | bytes 131104 | tf_op jit(solution)/shard_map/ppermute | solution.py:18
  59.9 4.4 %collective-permute-start.19 = (f32[2,4,4,8,256]{4,3,0,1,2:T(8,128)S(1)}, f32[2,4,4,8,256]{4,3,0,1,2:T(8,128)S(1)}, u32[]{:S(2)}, u32[]{:S(2)}) collective-permute-start(f32[2,4,4,8,256]{4,3,0,1,2:T(8,128)S(1)} %pad_maximum_fusion.2), channel_id=1, source_target_pairs={{0,24},{8,16},{16,8},{24,0},{1,25},{9,17},{17,9},{25,1},{2,26},{10... | collective-permute-start | bytes 786440 | tf_op jit(solution)/shard_map/ppermute | solution.py:18
  64.4 4.2 %collective-permute-done.19 = f32[2,4,4,8,256]{4,3,0,1,2:T(8,128)S(1)} collective-permute-done((f32[2,4,4,8,256]{4,3,0,1,2:T(8,128)S(1)}, f32[2,4,4,8,256]{4,3,0,1,2:T(8,128)S(1)}, u32[]{:S(2)}, u32[]{:S(2)}) %collective-permute-start.19) | collective-permute-done | bytes 262176 | tf_op jit(solution)/shard_map/ppermute | solution.py:18
  68.7 0.2 copy.10
  68.9 64.7 %all-to-all-done = f32[16,32,1024]{2,1,0:T(8,128)S(1)} async-done(((f32[16,32,1024]{2,1,0:T(8,128)}), f32[16,32,1024]{2,1,0:T(8,128)S(1)}, u32[]{:S(2)}, u32[]{:S(2)}) %all-to-all-start) | async-done | bytes 2097184 | tf_op jit(solution)/shard_map/all_to_all | solution.py:13
  133.6 2.1 fusion.7
  135.7 12.4 %all-to-all-start.1 = ((f32[16,16,1024]{2,1,0:T(8,128)}), f32[16,16,1024]{2,1,0:T(8,128)}, u32[]{:S(2)}, u32[]{:S(2)}) async-start(f32[16,16,1024]{2,1,0:T(8,128)} %fusion.7), calls=%async_computation.1 | async-start | bytes 2097152 | tf_op jit(solution)/shard_map/all_to_all | solution.py:13
  148.2 1.8 fusion.6
  150.1 3.2 %collective-permute-start.3 = (f32[512,256]{1,0:T(8,128)S(1)}, f32[512,256]{1,0:T(8,128)S(1)}, u32[]{:S(2)}, u32[]{:S(2)}) collective-permute-start(f32[512,256]{1,0:T(8,128)S(1)} %constant_dynamic-slice_fusion.12), channel_id=1, source_target_pairs={{0,1},{1,0},{2,3},{3,2},{4,5},{5,4},{6,7},{7,6},{8,9},{9,8},{10,11... | collective-permute-start | bytes 1572872 | tf_op jit(solution)/shard_map/ppermute | solution.py:18
  153.3 1.5 collective-permute-done.3
  154.8 0.1 dynamic-slice_add_fusion
  154.9 3.5 %collective-permute-start.4 = (f32[4,32,256]{2,1,0:T(8,128)S(1)}, f32[4,32,256]{2,1,0:T(8,128)S(1)}, u32[]{:S(2)}, u32[]{:S(2)}) collective-permute-start(f32[4,32,256]{2,1,0:T(8,128)S(1)} %get-tuple-element.18), channel_id=1, source_target_pairs={{0,32},{32,0},{64,96},{96,64},{1,33},{33,1},{65,97},{97,65},{2,34}... | collective-permute-start | bytes 393224 | tf_op jit(solution)/shard_map/ppermute | solution.py:18
  158.4 4.3 %collective-permute-start.5 = (f32[4,32,256]{2,1,0:T(8,128)S(1)}, f32[4,32,256]{2,1,0:T(8,128)S(1)}, u32[]{:S(2)}, u32[]{:S(2)}) collective-permute-start(f32[4,32,256]{2,1,0:T(8,128)S(1)} %get-tuple-element.17), channel_id=1, source_target_pairs={{0,64},{32,96},{64,0},{96,32},{1,65},{33,97},{65,1},{97,33},{2,66}... | collective-permute-start | bytes 393224 | tf_op jit(solution)/shard_map/ppermute | solution.py:18
  162.8 1.9 collective-permute-start.6
  164.7 0.0 collective-permute-done.4
  164.7 3.5 %collective-permute-done.5 = f32[4,32,256]{2,1,0:T(8,128)S(1)} collective-permute-done((f32[4,32,256]{2,1,0:T(8,128)S(1)}, f32[4,32,256]{2,1,0:T(8,128)S(1)}, u32[]{:S(2)}, u32[]{:S(2)}) %collective-permute-start.5) | collective-permute-done | bytes 131104 | tf_op jit(solution)/shard_map/ppermute | solution.py:18
  168.2 2.9 %collective-permute-done.6 = f32[4,32,256]{2,1,0:T(8,128)S(1)} collective-permute-done((f32[4,32,256]{2,1,0:T(8,128)S(1)}, f32[4,32,256]{2,1,0:T(8,128)S(1)}, u32[]{:S(2)}, u32[]{:S(2)}) %collective-permute-start.6) | collective-permute-done | bytes 131104 | tf_op jit(solution)/shard_map/ppermute | solution.py:18
  171.1 4.7 %collective-permute-start.8 = (f32[4,32,256]{2,1,0:T(8,128)S(1)}, f32[4,32,256]{2,1,0:T(8,128)S(1)}, u32[]{:S(2)}, u32[]{:S(2)}) collective-permute-start(f32[4,32,256]{2,1,0:T(8,128)S(1)} %fusion), channel_id=1, source_target_pairs={{0,16},{8,24},{16,0},{24,8},{1,17},{9,25},{17,1},{25,9},{2,18},{10... | collective-permute-start | bytes 393224 | tf_op jit(solution)/shard_map/ppermute | solution.py:18
  175.9 2.7 %collective-permute-start.9 = (f32[4,32,256]{2,1,0:T(8,128)S(1)}, f32[4,32,256]{2,1,0:T(8,128)S(1)}, u32[]{:S(2)}, u32[]{:S(2)}) collective-permute-start(f32[4,32,256]{2,1,0:T(8,128)S(1)} %fusion), channel_id=1, source_target_pairs={{0,24},{8,16},{16,8},{24,0},{1,25},{9,17},{17,9},{25,1},{2,26},{10... | collective-permute-start | bytes 393224 | tf_op jit(solution)/shard_map/ppermute | solution.py:18
  178.6 1.9 collective-permute-start.7
  180.5 0.0 collective-permute-done.8
  180.5 2.7 %collective-permute-done.9 = f32[4,32,256]{2,1,0:T(8,128)S(1)} collective-permute-done((f32[4,32,256]{2,1,0:T(8,128)S(1)}, f32[4,32,256]{2,1,0:T(8,128)S(1)}, u32[]{:S(2)}, u32[]{:S(2)}) %collective-permute-start.9) | collective-permute-done | bytes 131104 | tf_op jit(solution)/shard_map/ppermute | solution.py:18
  183.2 1.5 collective-permute-done.7
  184.7 6.7 %collective-permute-start.10 = (f32[32,256]{1,0:T(8,128)S(1)}, f32[32,256]{1,0:T(8,128)S(1)}, u32[]{:S(2)}, u32[]{:S(2)}) collective-permute-start(f32[32,256]{1,0:T(8,128)S(1)} %get-tuple-element.29), channel_id=1, source_target_pairs={{0,128},{128,0},{256,384},{384,256},{1,129},{129,1},{257,385},{385... | collective-permute-start | bytes 98312 | tf_op jit(solution)/shard_map/ppermute | solution.py:18
  191.5 7.8 %collective-permute-start.11 = (f32[32,256]{1,0:T(8,128)S(1)}, f32[32,256]{1,0:T(8,128)S(1)}, u32[]{:S(2)}, u32[]{:S(2)}) collective-permute-start(f32[32,256]{1,0:T(8,128)S(1)} %get-tuple-element.28), channel_id=1, source_target_pairs={{0,256},{128,384},{256,0},{384,128},{1,257},{129,385},{257,1},{385... | collective-permute-start | bytes 98312 | tf_op jit(solution)/shard_map/ppermute | solution.py:18
  199.3 1.9 collective-permute-start.12
  201.2 2.0 collective-permute-done.10
  203.3 1.6 collective-permute-done.11
  204.9 3.3 %collective-permute-done.12 = f32[32,256]{1,0:T(8,128)S(1)} collective-permute-done((f32[32,256]{1,0:T(8,128)S(1)}, f32[32,256]{1,0:T(8,128)S(1)}, u32[]{:S(2)}, u32[]{:S(2)}) %collective-permute-start.12) | collective-permute-done | bytes 32800 | tf_op jit(solution)/shard_map/ppermute | solution.py:18
  208.2 1.9 collective-permute-start.13
  210.1 2.7 %collective-permute-done.13 = f32[32,256]{1,0:T(8,128)S(1)} collective-permute-done((f32[32,256]{1,0:T(8,128)S(1)}, f32[32,256]{1,0:T(8,128)S(1)}, u32[]{:S(2)}, u32[]{:S(2)}) %collective-permute-start.13) | collective-permute-done | bytes 32800 | tf_op jit(solution)/shard_map/ppermute | solution.py:18
  212.8 5.5 %collective-permute-start.14 = (f32[32,256]{1,0:T(8,128)S(1)}, f32[32,256]{1,0:T(8,128)S(1)}, u32[]{:S(2)}, u32[]{:S(2)}) collective-permute-start(f32[32,256]{1,0:T(8,128)S(1)} %add.115), channel_id=1, source_target_pairs={{0,4},{2,6},{4,0},{6,2},{1,5},{3,7},{5,1},{7,3},{8,12},{10,14},{12... | collective-permute-start | bytes 98312 | tf_op jit(solution)/shard_map/ppermute | solution.py:18
  218.3 1.4 collective-permute-done.14
  219.7 6.9 %collective-permute-start.15 = (f32[32,256]{1,0:T(8,128)S(1)}, f32[32,256]{1,0:T(8,128)S(1)}, u32[]{:S(2)}, u32[]{:S(2)}) collective-permute-start(f32[32,256]{1,0:T(8,128)S(1)} %add.116), channel_id=1, source_target_pairs={{0,1},{1,0},{2,3},{3,2},{4,5},{5,4},{6,7},{7,6},{8,9},{9,8},{10,11... | collective-permute-start | bytes 98312 | tf_op jit(solution)/shard_map/ppermute | solution.py:18
  226.7 0.8 collective-permute-done.15
  227.5 0.6 pad_maximum_fusion.5
  228.1 0.0 all-to-all-done.1
  228.1 1.8 copy.11
  230.0 1.1 reshape.33
  (23 shorter events, 0.4 us)
Async XLA Ops:
  0.6 0.8 copy-start
  1.4 26.7 %collective-permute-start = (f32[8,256]{1,0:T(8,128)S(1)}, f32[8,256]{1,0:T(8,128)S(1)}, u32[]{:S(2)}, u32[]{:S(2)}) collective-permute-start(f32[8,256]{1,0:T(8,128)S(1)} %constant_dynamic-slice_fusion.13), channel_id=1, source_target_pairs={{0,128},{128,0},{256,384},{384,256},{1,129},{129,1},{257,385},{385... | collective-permute-start | bytes 24584 | tf_op jit(solution)/shard_map/ppermute | solution.py:18
  11.0 17.1 %collective-permute-start.1 = (f32[8,256]{1,0:T(8,128)S(1)}, f32[8,256]{1,0:T(8,128)S(1)}, u32[]{:S(2)}, u32[]{:S(2)}) collective-permute-start(f32[8,256]{1,0:T(8,128)S(1)} %constant_dynamic-slice_fusion.13), channel_id=1, source_target_pairs={{0,256},{128,384},{256,0},{384,128},{1,257},{129,385},{257,1},{385... | collective-permute-start | bytes 24584 | tf_op jit(solution)/shard_map/ppermute | solution.py:18
  21.7 8.3 %collective-permute-start.2 = (f32[8,256]{1,0:T(8,128)S(1)}, f32[8,256]{1,0:T(8,128)S(1)}, u32[]{:S(2)}, u32[]{:S(2)}) collective-permute-start(f32[8,256]{1,0:T(8,128)S(1)} %constant_dynamic-slice_fusion.13), channel_id=1, source_target_pairs={{0,384},{128,256},{256,128},{384,0},{1,385},{129,257},{257,129},{3... | collective-permute-start | bytes 24584 | tf_op jit(solution)/shard_map/ppermute | solution.py:18
  30.0 103.7 %all-to-all-start = ((f32[16,32,1024]{2,1,0:T(8,128)}), f32[16,32,1024]{2,1,0:T(8,128)S(1)}, u32[]{:S(2)}, u32[]{:S(2)}) async-start(f32[16,32,1024]{2,1,0:T(8,128)} %bitcast.56), calls=%async_computation | async-start | bytes 4194304 | tf_op jit(solution)/shard_map/all_to_all | solution.py:13
  40.6 6.7 %collective-permute-start.16 = (f32[4,8,256]{2,1,0:T(8,128)S(1)}, f32[4,8,256]{2,1,0:T(8,128)S(1)}, u32[]{:S(2)}, u32[]{:S(2)}) collective-permute-start(f32[4,8,256]{2,1,0:T(8,128)S(1)} %get-tuple-element.35), channel_id=1, source_target_pairs={{0,32},{32,0},{64,96},{96,64},{1,33},{33,1},{65,97},{97,65},{2,34}... | collective-permute-start | bytes 98312 | tf_op jit(solution)/shard_map/ppermute | solution.py:18
  47.3 6.5 %collective-permute-start.17 = (f32[2,4,8,256]{3,2,0,1:T(8,128)S(1)}, f32[2,4,8,256]{3,2,0,1:T(8,128)S(1)}, u32[]{:S(2)}, u32[]{:S(2)}) collective-permute-start(f32[2,4,8,256]{3,2,0,1:T(8,128)S(1)} %pad_maximum_fusion.6), channel_id=1, source_target_pairs={{0,96},{32,64},{64,32},{96,0},{1,97},{33,65},{65,33},{97,1},{2,98}... | collective-permute-start | bytes 196616 | tf_op jit(solution)/shard_map/ppermute | solution.py:18
  53.9 6.0 %collective-permute-start.18 = (f32[4,4,8,256]{3,2,0,1:T(8,128)S(1)}, f32[4,4,8,256]{3,2,0,1:T(8,128)S(1)}, u32[]{:S(2)}, u32[]{:S(2)}) collective-permute-start(f32[4,4,8,256]{3,2,0,1:T(8,128)S(1)} %get-tuple-element.22), channel_id=1, source_target_pairs={{0,8},{8,0},{16,24},{24,16},{1,9},{9,1},{17,25},{25,17},{2,10},{10... | collective-permute-start | bytes 393224 | tf_op jit(solution)/shard_map/ppermute | solution.py:18
  59.9 8.6 %collective-permute-start.19 = (f32[2,4,4,8,256]{4,3,0,1,2:T(8,128)S(1)}, f32[2,4,4,8,256]{4,3,0,1,2:T(8,128)S(1)}, u32[]{:S(2)}, u32[]{:S(2)}) collective-permute-start(f32[2,4,4,8,256]{4,3,0,1,2:T(8,128)S(1)} %pad_maximum_fusion.2), channel_id=1, source_target_pairs={{0,24},{8,16},{16,8},{24,0},{1,25},{9,17},{17,9},{25,1},{2,26},{10... | collective-permute-start | bytes 786440 | tf_op jit(solution)/shard_map/ppermute | solution.py:18
  135.7 92.4 %all-to-all-start.1 = ((f32[16,16,1024]{2,1,0:T(8,128)}), f32[16,16,1024]{2,1,0:T(8,128)}, u32[]{:S(2)}, u32[]{:S(2)}) async-start(f32[16,16,1024]{2,1,0:T(8,128)} %fusion.7), calls=%async_computation.1 | async-start | bytes 2097152 | tf_op jit(solution)/shard_map/all_to_all | solution.py:13
  150.1 4.7 %collective-permute-start.3 = (f32[512,256]{1,0:T(8,128)S(1)}, f32[512,256]{1,0:T(8,128)S(1)}, u32[]{:S(2)}, u32[]{:S(2)}) collective-permute-start(f32[512,256]{1,0:T(8,128)S(1)} %constant_dynamic-slice_fusion.12), channel_id=1, source_target_pairs={{0,1},{1,0},{2,3},{3,2},{4,5},{5,4},{6,7},{7,6},{8,9},{9,8},{10,11... | collective-permute-start | bytes 1572872 | tf_op jit(solution)/shard_map/ppermute | solution.py:18
  154.9 9.7 %collective-permute-start.4 = (f32[4,32,256]{2,1,0:T(8,128)S(1)}, f32[4,32,256]{2,1,0:T(8,128)S(1)}, u32[]{:S(2)}, u32[]{:S(2)}) collective-permute-start(f32[4,32,256]{2,1,0:T(8,128)S(1)} %get-tuple-element.18), channel_id=1, source_target_pairs={{0,32},{32,0},{64,96},{96,64},{1,33},{33,1},{65,97},{97,65},{2,34}... | collective-permute-start | bytes 393224 | tf_op jit(solution)/shard_map/ppermute | solution.py:18
  158.4 9.7 %collective-permute-start.5 = (f32[4,32,256]{2,1,0:T(8,128)S(1)}, f32[4,32,256]{2,1,0:T(8,128)S(1)}, u32[]{:S(2)}, u32[]{:S(2)}) collective-permute-start(f32[4,32,256]{2,1,0:T(8,128)S(1)} %get-tuple-element.17), channel_id=1, source_target_pairs={{0,64},{32,96},{64,0},{96,32},{1,65},{33,97},{65,1},{97,33},{2,66}... | collective-permute-start | bytes 393224 | tf_op jit(solution)/shard_map/ppermute | solution.py:18
  162.8 8.3 %collective-permute-start.6 = (f32[4,32,256]{2,1,0:T(8,128)S(1)}, f32[4,32,256]{2,1,0:T(8,128)S(1)}, u32[]{:S(2)}, u32[]{:S(2)}) collective-permute-start(f32[4,32,256]{2,1,0:T(8,128)S(1)} %get-tuple-element.16), channel_id=1, source_target_pairs={{0,96},{32,64},{64,32},{96,0},{1,97},{33,65},{65,33},{97,1},{2,98}... | collective-permute-start | bytes 393224 | tf_op jit(solution)/shard_map/ppermute | solution.py:18
  171.1 9.4 %collective-permute-start.8 = (f32[4,32,256]{2,1,0:T(8,128)S(1)}, f32[4,32,256]{2,1,0:T(8,128)S(1)}, u32[]{:S(2)}, u32[]{:S(2)}) collective-permute-start(f32[4,32,256]{2,1,0:T(8,128)S(1)} %fusion), channel_id=1, source_target_pairs={{0,16},{8,24},{16,0},{24,8},{1,17},{9,25},{17,1},{25,9},{2,18},{10... | collective-permute-start | bytes 393224 | tf_op jit(solution)/shard_map/ppermute | solution.py:18
  175.9 7.3 %collective-permute-start.9 = (f32[4,32,256]{2,1,0:T(8,128)S(1)}, f32[4,32,256]{2,1,0:T(8,128)S(1)}, u32[]{:S(2)}, u32[]{:S(2)}) collective-permute-start(f32[4,32,256]{2,1,0:T(8,128)S(1)} %fusion), channel_id=1, source_target_pairs={{0,24},{8,16},{16,8},{24,0},{1,25},{9,17},{17,9},{25,1},{2,26},{10... | collective-permute-start | bytes 393224 | tf_op jit(solution)/shard_map/ppermute | solution.py:18
  178.6 6.1 %collective-permute-start.7 = (f32[4,32,256]{2,1,0:T(8,128)S(1)}, f32[4,32,256]{2,1,0:T(8,128)S(1)}, u32[]{:S(2)}, u32[]{:S(2)}) collective-permute-start(f32[4,32,256]{2,1,0:T(8,128)S(1)} %fusion), channel_id=1, source_target_pairs={{0,8},{8,0},{16,24},{24,16},{1,9},{9,1},{17,25},{25,17},{2,10},{10... | collective-permute-start | bytes 393224 | tf_op jit(solution)/shard_map/ppermute | solution.py:18
  184.7 18.5 %collective-permute-start.10 = (f32[32,256]{1,0:T(8,128)S(1)}, f32[32,256]{1,0:T(8,128)S(1)}, u32[]{:S(2)}, u32[]{:S(2)}) collective-permute-start(f32[32,256]{1,0:T(8,128)S(1)} %get-tuple-element.29), channel_id=1, source_target_pairs={{0,128},{128,0},{256,384},{384,256},{1,129},{129,1},{257,385},{385... | collective-permute-start | bytes 98312 | tf_op jit(solution)/shard_map/ppermute | solution.py:18
  191.5 13.4 %collective-permute-start.11 = (f32[32,256]{1,0:T(8,128)S(1)}, f32[32,256]{1,0:T(8,128)S(1)}, u32[]{:S(2)}, u32[]{:S(2)}) collective-permute-start(f32[32,256]{1,0:T(8,128)S(1)} %get-tuple-element.28), channel_id=1, source_target_pairs={{0,256},{128,384},{256,0},{384,128},{1,257},{129,385},{257,1},{385... | collective-permute-start | bytes 98312 | tf_op jit(solution)/shard_map/ppermute | solution.py:18
  199.3 8.9 %collective-permute-start.12 = (f32[32,256]{1,0:T(8,128)S(1)}, f32[32,256]{1,0:T(8,128)S(1)}, u32[]{:S(2)}, u32[]{:S(2)}) collective-permute-start(f32[32,256]{1,0:T(8,128)S(1)} %get-tuple-element.27), channel_id=1, source_target_pairs={{0,384},{128,256},{256,128},{384,0},{1,385},{129,257},{257,129},{3... | collective-permute-start | bytes 98312 | tf_op jit(solution)/shard_map/ppermute | solution.py:18
  208.2 4.7 %collective-permute-start.13 = (f32[32,256]{1,0:T(8,128)S(1)}, f32[32,256]{1,0:T(8,128)S(1)}, u32[]{:S(2)}, u32[]{:S(2)}) collective-permute-start(f32[32,256]{1,0:T(8,128)S(1)} %fusion.1), channel_id=1, source_target_pairs={{0,2},{2,0},{4,6},{6,4},{1,3},{3,1},{5,7},{7,5},{8,10},{10,8},{12,... | collective-permute-start | bytes 98312 | tf_op jit(solution)/shard_map/ppermute | solution.py:18
  212.8 6.9 %collective-permute-start.14 = (f32[32,256]{1,0:T(8,128)S(1)}, f32[32,256]{1,0:T(8,128)S(1)}, u32[]{:S(2)}, u32[]{:S(2)}) collective-permute-start(f32[32,256]{1,0:T(8,128)S(1)} %add.115), channel_id=1, source_target_pairs={{0,4},{2,6},{4,0},{6,2},{1,5},{3,7},{5,1},{7,3},{8,12},{10,14},{12... | collective-permute-start | bytes 98312 | tf_op jit(solution)/shard_map/ppermute | solution.py:18
  219.7 7.8 %collective-permute-start.15 = (f32[32,256]{1,0:T(8,128)S(1)}, f32[32,256]{1,0:T(8,128)S(1)}, u32[]{:S(2)}, u32[]{:S(2)}) collective-permute-start(f32[32,256]{1,0:T(8,128)S(1)} %add.116), channel_id=1, source_target_pairs={{0,1},{1,0},{2,3},{3,2},{4,5},{5,4},{6,7},{7,6},{8,9},{9,8},{10,11... | collective-permute-start | bytes 98312 | tf_op jit(solution)/shard_map/ppermute | solution.py:18

commit v3 on v2

--- a/solution.py
+++ b/solution.py
@@ -47,11 +47,11 @@
 def gather_zh(factor):
     rows = factor.shape[0] // 4
     part = lax.dynamic_slice_in_dim(factor, lax.axis_index("x") * rows, rows, 0)
-    return [part] + [swap(part, "zh", k) for k in (1, 2, 3)]
+    return lax.all_gather(part, "zh")
 
 
 def spread_factor(parts):
-    parts = gather(gather(by_owner(parts, lax.axis_index("zh")), "y"), "x")
+    parts = gather(gather(parts, "y"), "x")
     return parts.transpose(2, 1, 0, 3, 4).reshape(-1, parts.shape[-1])
 
 

time: 232 us -> 229 us (0.987)
  blocking collectives: 0 us -> 23.7 us
  starting transfers between devices: 113 us -> 91.2 us
  waiting for transfers between devices: 104 us -> 100 us
    all_gather x0 -> x1, blocking collectives: none -> 23.7 us  [gather_zh(): return lax.all_gather(part, 'zh')]
    ppermute x20 -> x17, starting transfers between devices: 89.7 us -> 70.1 us  [swap(): return lax.ppermute(value, axis, [(i, i ^ flip) for i in range(count)])]
    ppermute x20 -> x17, waiting for transfers between devices: 39.1 us -> 33.9 us  [swap(): return lax.ppermute(value, axis, [(i, i ^ flip) for i in range(count)])]
  transfers between devices with their start and end apart: 22 -> 19, of which waited for: 17 -> 15; matrix products, arithmetic and copies ran while one was open for 3% -> 1% of each run, Pallas kernels for 0% -> 0%
where the time goes in v3:
time: 229 us
  waiting for transfers between devices  100 us (44%)
  starting transfers between devices  91.2 us (40%)
  blocking collectives  23.7 us (10%)
  local copies, waits for them, and re-layouts  7.85 us (3%)
  matrix products  3.9 us (2%)
    ppermute x17, starting transfers between devices, swap(): return lax.ppermute(value, axis, [(i, i ^ flip) for i in range(count)])  70.1 us
    all_to_all x2, waiting for transfers between devices, exchange(): return lax.all_to_all(value, axis, split_axis=0, concat_axis=0, tiled=True)  66.1 us
    ppermute x17, waiting for transfers between devices, swap(): return lax.ppermute(value, axis, [(i, i ^ flip) for i in range(count)])  33.9 us
    all_gather x1, blocking collectives, gather_zh(): return lax.all_gather(part, 'zh')  23.7 us
    all_to_all x2, starting transfers between devices, exchange(): return lax.all_to_all(value, axis, split_axis=0, concat_axis=0, tiled=True)  21.1 us
  transfers between devices with their start and end apart: 19, of which 15 were waited for; matrix products, arithmetic and copies ran while one was open for 1% of the time, Pallas kernels for 0%

profile of v3, /device:TPU:1, one launch (start us, length us, event | category | flops | bytes accessed | tf_op | source)
XLA Modules:
  0.0 228.6 jit_solution(14490432547406025632)
XLA Ops:
  0.6 0.0 copy-start
  0.6 1.9 reshape.29
  2.6 2.6 %copy.14 = f32[32,16,1024]{2,0,1:T(8,128)} copy(f32[32,16,1024]{2,1,0:T(8,128)S(1)} %reshape.29) | data formatting | bytes 4194304 | tf_op jit(solution)/shard_map/reshape | solution.py:80
  5.1 0.0 copy-done
  5.2 23.7 %all-gather = f32[32,256]{1,0:T(8,128)S(1)} all-gather(f32[8,256]{1,0:T(8,128)S(1)} %constant_dynamic-slice_fusion.9), channel_id=2, replica_groups=mesh['zh'=4,'y'=4,'x'=4,'zl'=4,'core'=2] {'zh'}, dimensions={0}, use_global_device_ids=true | all-gather | bytes 40960 | tf_op jit(solution)/shard_map/all_gather | solution.py:50
  28.8 9.1 %all-to-all-start = ((f32[16,32,1024]{2,1,0:T(8,128)}), f32[16,32,1024]{2,1,0:T(8,128)S(1)}, u32[]{:S(2)}, u32[]{:S(2)}) async-start(f32[16,32,1024]{2,1,0:T(8,128)} %bitcast.52), calls=%async_computation | async-start | bytes 4194304 | tf_op jit(solution)/shard_map/all_to_all | solution.py:13
  37.9 3.3 %collective-permute-start.13 = (f32[4,8,256]{2,1,0:T(8,128)S(1)}, f32[4,8,256]{2,1,0:T(8,128)S(1)}, u32[]{:S(2)}, u32[]{:S(2)}) collective-permute-start(f32[4,8,256]{2,1,0:T(8,128)S(1)} %bitcast.59), channel_id=1, source_target_pairs={{0,32},{32,0},{64,96},{96,64},{1,33},{33,1},{65,97},{97,65},{2,34}... | collective-permute-start | bytes 98312 | tf_op jit(solution)/shard_map/ppermute | solution.py:18
  41.2 2.4 %collective-permute-done.13 = f32[4,8,256]{2,1,0:T(8,128)S(1)} collective-permute-done((f32[4,8,256]{2,1,0:T(8,128)S(1)}, f32[4,8,256]{2,1,0:T(8,128)S(1)}, u32[]{:S(2)}, u32[]{:S(2)}) %collective-permute-start.13) | collective-permute-done | bytes 32800 | tf_op jit(solution)/shard_map/ppermute | solution.py:18
  43.6 3.7 %collective-permute-start.14 = (f32[2,4,8,256]{3,2,0,1:T(8,128)S(1)}, f32[2,4,8,256]{3,2,0,1:T(8,128)S(1)}, u32[]{:S(2)}, u32[]{:S(2)}) collective-permute-start(f32[2,4,8,256]{3,2,0,1:T(8,128)S(1)} %pad_maximum_fusion.6), channel_id=1, source_target_pairs={{0,96},{32,64},{64,32},{96,0},{1,97},{33,65},{65,33},{97,1},{2,98}... | collective-permute-start | bytes 196616 | tf_op jit(solution)/shard_map/ppermute | solution.py:18
  47.4 3.0 %collective-permute-done.14 = f32[2,4,8,256]{3,2,0,1:T(8,128)S(1)} collective-permute-done((f32[2,4,8,256]{3,2,0,1:T(8,128)S(1)}, f32[2,4,8,256]{3,2,0,1:T(8,128)S(1)}, u32[]{:S(2)}, u32[]{:S(2)}) %collective-permute-start.14) | collective-permute-done | bytes 65568 | tf_op jit(solution)/shard_map/ppermute | solution.py:18
  50.4 3.1 %collective-permute-start.15 = (f32[4,4,8,256]{3,2,0,1:T(8,128)S(1)}, f32[4,4,8,256]{3,2,0,1:T(8,128)S(1)}, u32[]{:S(2)}, u32[]{:S(2)}) collective-permute-start(f32[4,4,8,256]{3,2,0,1:T(8,128)S(1)} %get-tuple-element.16), channel_id=1, source_target_pairs={{0,8},{8,0},{16,24},{24,16},{1,9},{9,1},{17,25},{25,17},{2,10},{10... | collective-permute-start | bytes 393224 | tf_op jit(solution)/shard_map/ppermute | solution.py:18
  53.5 2.9 %collective-permute-done.15 = f32[4,4,8,256]{3,2,0,1:T(8,128)S(1)} collective-permute-done((f32[4,4,8,256]{3,2,0,1:T(8,128)S(1)}, f32[4,4,8,256]{3,2,0,1:T(8,128)S(1)}, u32[]{:S(2)}, u32[]{:S(2)}) %collective-permute-start.15) | collective-permute-done | bytes 131104 | tf_op jit(solution)/shard_map/ppermute | solution.py:18
  56.4 4.4 %collective-permute-start.16 = (f32[2,4,4,8,256]{4,3,0,1,2:T(8,128)S(1)}, f32[2,4,4,8,256]{4,3,0,1,2:T(8,128)S(1)}, u32[]{:S(2)}, u32[]{:S(2)}) collective-permute-start(f32[2,4,4,8,256]{4,3,0,1,2:T(8,128)S(1)} %pad_maximum_fusion.2), channel_id=1, source_target_pairs={{0,24},{8,16},{16,8},{24,0},{1,25},{9,17},{17,9},{25,1},{2,26},{10... | collective-permute-start | bytes 786440 | tf_op jit(solution)/shard_map/ppermute | solution.py:18
  60.9 4.2 %collective-permute-done.16 = f32[2,4,4,8,256]{4,3,0,1,2:T(8,128)S(1)} collective-permute-done((f32[2,4,4,8,256]{4,3,0,1,2:T(8,128)S(1)}, f32[2,4,4,8,256]{4,3,0,1,2:T(8,128)S(1)}, u32[]{:S(2)}, u32[]{:S(2)}) %collective-permute-start.16) | collective-permute-done | bytes 262176 | tf_op jit(solution)/shard_map/ppermute | solution.py:18
  65.2 0.2 copy.11
  65.4 66.1 %all-to-all-done = f32[16,32,1024]{2,1,0:T(8,128)S(1)} async-done(((f32[16,32,1024]{2,1,0:T(8,128)}), f32[16,32,1024]{2,1,0:T(8,128)S(1)}, u32[]{:S(2)}, u32[]{:S(2)}) %all-to-all-start) | async-done | bytes 2097184 | tf_op jit(solution)/shard_map/all_to_all | solution.py:13
  131.5 2.1 fusion.6
  133.6 12.0 %all-to-all-start.1 = ((f32[16,16,1024]{2,1,0:T(8,128)}), f32[16,16,1024]{2,1,0:T(8,128)}, u32[]{:S(2)}, u32[]{:S(2)}) async-start(f32[16,16,1024]{2,1,0:T(8,128)} %fusion.6), calls=%async_computation.1 | async-start | bytes 2097152 | tf_op jit(solution)/shard_map/all_to_all | solution.py:13
  145.6 1.8 fusion.5
  147.5 3.2 %collective-permute-start = (f32[512,256]{1,0:T(8,128)S(1)}, f32[512,256]{1,0:T(8,128)S(1)}, u32[]{:S(2)}, u32[]{:S(2)}) collective-permute-start(f32[512,256]{1,0:T(8,128)S(1)} %constant_dynamic-slice_fusion.8), channel_id=1, source_target_pairs={{0,1},{1,0},{2,3},{3,2},{4,5},{5,4},{6,7},{7,6},{8,9},{9,8},{10,11... | collective-permute-start | bytes 1572872 | tf_op jit(solution)/shard_map/ppermute | solution.py:18
  150.7 1.5 collective-permute-done
  152.2 0.1 dynamic-slice_add_fusion
  152.4 3.5 %collective-permute-start.1 = (f32[4,32,256]{2,1,0:T(8,128)S(1)}, f32[4,32,256]{2,1,0:T(8,128)S(1)}, u32[]{:S(2)}, u32[]{:S(2)}) collective-permute-start(f32[4,32,256]{2,1,0:T(8,128)S(1)} %get-tuple-element.12), channel_id=1, source_target_pairs={{0,32},{32,0},{64,96},{96,64},{1,33},{33,1},{65,97},{97,65},{2,34}... | collective-permute-start | bytes 393224 | tf_op jit(solution)/shard_map/ppermute | solution.py:18
  155.9 4.3 %collective-permute-start.2 = (f32[4,32,256]{2,1,0:T(8,128)S(1)}, f32[4,32,256]{2,1,0:T(8,128)S(1)}, u32[]{:S(2)}, u32[]{:S(2)}) collective-permute-start(f32[4,32,256]{2,1,0:T(8,128)S(1)} %get-tuple-element.11), channel_id=1, source_target_pairs={{0,64},{32,96},{64,0},{96,32},{1,65},{33,97},{65,1},{97,33},{2,66}... | collective-permute-start | bytes 393224 | tf_op jit(solution)/shard_map/ppermute | solution.py:18
  160.2 1.9 collective-permute-start.3
  162.1 0.0 collective-permute-done.1
  162.2 3.0 %collective-permute-done.2 = f32[4,32,256]{2,1,0:T(8,128)S(1)} collective-permute-done((f32[4,32,256]{2,1,0:T(8,128)S(1)}, f32[4,32,256]{2,1,0:T(8,128)S(1)}, u32[]{:S(2)}, u32[]{:S(2)}) %collective-permute-start.2) | collective-permute-done | bytes 131104 | tf_op jit(solution)/shard_map/ppermute | solution.py:18
  165.1 2.4 %collective-permute-done.3 = f32[4,32,256]{2,1,0:T(8,128)S(1)} collective-permute-done((f32[4,32,256]{2,1,0:T(8,128)S(1)}, f32[4,32,256]{2,1,0:T(8,128)S(1)}, u32[]{:S(2)}, u32[]{:S(2)}) %collective-permute-start.3) | collective-permute-done | bytes 131104 | tf_op jit(solution)/shard_map/ppermute | solution.py:18
  167.6 4.7 %collective-permute-start.5 = (f32[4,32,256]{2,1,0:T(8,128)S(1)}, f32[4,32,256]{2,1,0:T(8,128)S(1)}, u32[]{:S(2)}, u32[]{:S(2)}) collective-permute-start(f32[4,32,256]{2,1,0:T(8,128)S(1)} %fusion), channel_id=1, source_target_pairs={{0,16},{8,24},{16,0},{24,8},{1,17},{9,25},{17,1},{25,9},{2,18},{10... | collective-permute-start | bytes 393224 | tf_op jit(solution)/shard_map/ppermute | solution.py:18
  172.2 2.8 %collective-permute-start.6 = (f32[4,32,256]{2,1,0:T(8,128)S(1)}, f32[4,32,256]{2,1,0:T(8,128)S(1)}, u32[]{:S(2)}, u32[]{:S(2)}) collective-permute-start(f32[4,32,256]{2,1,0:T(8,128)S(1)} %fusion), channel_id=1, source_target_pairs={{0,24},{8,16},{16,8},{24,0},{1,25},{9,17},{17,9},{25,1},{2,26},{10... | collective-permute-start | bytes 393224 | tf_op jit(solution)/shard_map/ppermute | solution.py:18
  175.0 1.9 collective-permute-start.4
  177.0 0.0 collective-permute-done.5
  177.0 2.6 %collective-permute-done.6 = f32[4,32,256]{2,1,0:T(8,128)S(1)} collective-permute-done((f32[4,32,256]{2,1,0:T(8,128)S(1)}, f32[4,32,256]{2,1,0:T(8,128)S(1)}, u32[]{:S(2)}, u32[]{:S(2)}) %collective-permute-start.6) | collective-permute-done | bytes 131104 | tf_op jit(solution)/shard_map/ppermute | solution.py:18
  179.6 1.6 collective-permute-done.4
  181.2 7.1 %collective-permute-start.7 = (f32[32,256]{1,0:T(8,128)S(1)}, f32[32,256]{1,0:T(8,128)S(1)}, u32[]{:S(2)}, u32[]{:S(2)}) collective-permute-start(f32[32,256]{1,0:T(8,128)S(1)} %get-tuple-element.23), channel_id=1, source_target_pairs={{0,128},{128,0},{256,384},{384,256},{1,129},{129,1},{257,385},{385... | collective-permute-start | bytes 98312 | tf_op jit(solution)/shard_map/ppermute | solution.py:18
  188.3 6.9 %collective-permute-start.8 = (f32[32,256]{1,0:T(8,128)S(1)}, f32[32,256]{1,0:T(8,128)S(1)}, u32[]{:S(2)}, u32[]{:S(2)}) collective-permute-start(f32[32,256]{1,0:T(8,128)S(1)} %get-tuple-element.22), channel_id=1, source_target_pairs={{0,256},{128,384},{256,0},{384,128},{1,257},{129,385},{257,1},{385... | collective-permute-start | bytes 98312 | tf_op jit(solution)/shard_map/ppermute | solution.py:18
  195.2 2.2 collective-permute-start.9
  197.4 0.0 collective-permute-done.7
  197.4 4.2 %collective-permute-done.8 = f32[32,256]{1,0:T(8,128)S(1)} collective-permute-done((f32[32,256]{1,0:T(8,128)S(1)}, f32[32,256]{1,0:T(8,128)S(1)}, u32[]{:S(2)}, u32[]{:S(2)}) %collective-permute-start.8) | collective-permute-done | bytes 32800 | tf_op jit(solution)/shard_map/ppermute | solution.py:18
  201.7 2.8 %collective-permute-done.9 = f32[32,256]{1,0:T(8,128)S(1)} collective-permute-done((f32[32,256]{1,0:T(8,128)S(1)}, f32[32,256]{1,0:T(8,128)S(1)}, u32[]{:S(2)}, u32[]{:S(2)}) %collective-permute-start.9) | collective-permute-done | bytes 32800 | tf_op jit(solution)/shard_map/ppermute | solution.py:18
  204.4 4.4 %collective-permute-start.10 = (f32[32,256]{1,0:T(8,128)S(1)}, f32[32,256]{1,0:T(8,128)S(1)}, u32[]{:S(2)}, u32[]{:S(2)}) collective-permute-start(f32[32,256]{1,0:T(8,128)S(1)} %fusion.1), channel_id=1, source_target_pairs={{0,2},{2,0},{4,6},{6,4},{1,3},{3,1},{5,7},{7,5},{8,10},{10,8},{12,... | collective-permute-start | bytes 98312 | tf_op jit(solution)/shard_map/ppermute | solution.py:18
  208.8 1.3 collective-permute-done.10
  210.1 4.9 %collective-permute-start.11 = (f32[32,256]{1,0:T(8,128)S(1)}, f32[32,256]{1,0:T(8,128)S(1)}, u32[]{:S(2)}, u32[]{:S(2)}) collective-permute-start(f32[32,256]{1,0:T(8,128)S(1)} %add.110), channel_id=1, source_target_pairs={{0,4},{2,6},{4,0},{6,2},{1,5},{3,7},{5,1},{7,3},{8,12},{10,14},{12... | collective-permute-start | bytes 98312 | tf_op jit(solution)/shard_map/ppermute | solution.py:18
  215.1 1.3 collective-permute-done.11
  216.4 7.8 %collective-permute-start.12 = (f32[32,256]{1,0:T(8,128)S(1)}, f32[32,256]{1,0:T(8,128)S(1)}, u32[]{:S(2)}, u32[]{:S(2)}) collective-permute-start(f32[32,256]{1,0:T(8,128)S(1)} %add.111), channel_id=1, source_target_pairs={{0,1},{1,0},{2,3},{3,2},{4,5},{5,4},{6,7},{7,6},{8,9},{9,8},{10,11... | collective-permute-start | bytes 98312 | tf_op jit(solution)/shard_map/ppermute | solution.py:18
  224.2 0.8 collective-permute-done.12
  225.0 0.6 pad_maximum_fusion.5
  225.6 0.0 all-to-all-done.1
  225.6 1.8 copy.12
  227.5 1.1 reshape.33
  (20 shorter events, 0.4 us)
Async XLA Ops:
  0.6 4.5 %copy-start = (f32[32,256]{1,0:T(8,128)S(1)}, f32[32,256]{1,0:T(8,128)}, u32[]{:S(2)}) copy-start(f32[32,256]{1,0:T(8,128)} %param.3) | copy-start | bytes 98308
  28.8 102.7 %all-to-all-start = ((f32[16,32,1024]{2,1,0:T(8,128)}), f32[16,32,1024]{2,1,0:T(8,128)S(1)}, u32[]{:S(2)}, u32[]{:S(2)}) async-start(f32[16,32,1024]{2,1,0:T(8,128)} %bitcast.52), calls=%async_computation | async-start | bytes 4194304 | tf_op jit(solution)/shard_map/all_to_all | solution.py:13
  37.9 5.7 %collective-permute-start.13 = (f32[4,8,256]{2,1,0:T(8,128)S(1)}, f32[4,8,256]{2,1,0:T(8,128)S(1)}, u32[]{:S(2)}, u32[]{:S(2)}) collective-permute-start(f32[4,8,256]{2,1,0:T(8,128)S(1)} %bitcast.59), channel_id=1, source_target_pairs={{0,32},{32,0},{64,96},{96,64},{1,33},{33,1},{65,97},{97,65},{2,34}... | collective-permute-start | bytes 98312 | tf_op jit(solution)/shard_map/ppermute | solution.py:18
  43.6 6.7 %collective-permute-start.14 = (f32[2,4,8,256]{3,2,0,1:T(8,128)S(1)}, f32[2,4,8,256]{3,2,0,1:T(8,128)S(1)}, u32[]{:S(2)}, u32[]{:S(2)}) collective-permute-start(f32[2,4,8,256]{3,2,0,1:T(8,128)S(1)} %pad_maximum_fusion.6), channel_id=1, source_target_pairs={{0,96},{32,64},{64,32},{96,0},{1,97},{33,65},{65,33},{97,1},{2,98}... | collective-permute-start | bytes 196616 | tf_op jit(solution)/shard_map/ppermute | solution.py:18
  50.4 6.0 %collective-permute-start.15 = (f32[4,4,8,256]{3,2,0,1:T(8,128)S(1)}, f32[4,4,8,256]{3,2,0,1:T(8,128)S(1)}, u32[]{:S(2)}, u32[]{:S(2)}) collective-permute-start(f32[4,4,8,256]{3,2,0,1:T(8,128)S(1)} %get-tuple-element.16), channel_id=1, source_target_pairs={{0,8},{8,0},{16,24},{24,16},{1,9},{9,1},{17,25},{25,17},{2,10},{10... | collective-permute-start | bytes 393224 | tf_op jit(solution)/shard_map/ppermute | solution.py:18
  56.4 8.6 %collective-permute-start.16 = (f32[2,4,4,8,256]{4,3,0,1,2:T(8,128)S(1)}, f32[2,4,4,8,256]{4,3,0,1,2:T(8,128)S(1)}, u32[]{:S(2)}, u32[]{:S(2)}) collective-permute-start(f32[2,4,4,8,256]{4,3,0,1,2:T(8,128)S(1)} %pad_maximum_fusion.2), channel_id=1, source_target_pairs={{0,24},{8,16},{16,8},{24,0},{1,25},{9,17},{17,9},{25,1},{2,26},{10... | collective-permute-start | bytes 786440 | tf_op jit(solution)/shard_map/ppermute | solution.py:18
  133.6 92.1 %all-to-all-start.1 = ((f32[16,16,1024]{2,1,0:T(8,128)}), f32[16,16,1024]{2,1,0:T(8,128)}, u32[]{:S(2)}, u32[]{:S(2)}) async-start(f32[16,16,1024]{2,1,0:T(8,128)} %fusion.6), calls=%async_computation.1 | async-start | bytes 2097152 | tf_op jit(solution)/shard_map/all_to_all | solution.py:13
  147.5 4.8 %collective-permute-start = (f32[512,256]{1,0:T(8,128)S(1)}, f32[512,256]{1,0:T(8,128)S(1)}, u32[]{:S(2)}, u32[]{:S(2)}) collective-permute-start(f32[512,256]{1,0:T(8,128)S(1)} %constant_dynamic-slice_fusion.8), channel_id=1, source_target_pairs={{0,1},{1,0},{2,3},{3,2},{4,5},{5,4},{6,7},{7,6},{8,9},{9,8},{10,11... | collective-permute-start | bytes 1572872 | tf_op jit(solution)/shard_map/ppermute | solution.py:18
  152.4 9.7 %collective-permute-start.1 = (f32[4,32,256]{2,1,0:T(8,128)S(1)}, f32[4,32,256]{2,1,0:T(8,128)S(1)}, u32[]{:S(2)}, u32[]{:S(2)}) collective-permute-start(f32[4,32,256]{2,1,0:T(8,128)S(1)} %get-tuple-element.12), channel_id=1, source_target_pairs={{0,32},{32,0},{64,96},{96,64},{1,33},{33,1},{65,97},{97,65},{2,34}... | collective-permute-start | bytes 393224 | tf_op jit(solution)/shard_map/ppermute | solution.py:18
  155.9 9.2 %collective-permute-start.2 = (f32[4,32,256]{2,1,0:T(8,128)S(1)}, f32[4,32,256]{2,1,0:T(8,128)S(1)}, u32[]{:S(2)}, u32[]{:S(2)}) collective-permute-start(f32[4,32,256]{2,1,0:T(8,128)S(1)} %get-tuple-element.11), channel_id=1, source_target_pairs={{0,64},{32,96},{64,0},{96,32},{1,65},{33,97},{65,1},{97,33},{2,66}... | collective-permute-start | bytes 393224 | tf_op jit(solution)/shard_map/ppermute | solution.py:18
  160.2 7.3 %collective-permute-start.3 = (f32[4,32,256]{2,1,0:T(8,128)S(1)}, f32[4,32,256]{2,1,0:T(8,128)S(1)}, u32[]{:S(2)}, u32[]{:S(2)}) collective-permute-start(f32[4,32,256]{2,1,0:T(8,128)S(1)} %get-tuple-element.10), channel_id=1, source_target_pairs={{0,96},{32,64},{64,32},{96,0},{1,97},{33,65},{65,33},{97,1},{2,98}... | collective-permute-start | bytes 393224 | tf_op jit(solution)/shard_map/ppermute | solution.py:18
  167.6 9.4 %collective-permute-start.5 = (f32[4,32,256]{2,1,0:T(8,128)S(1)}, f32[4,32,256]{2,1,0:T(8,128)S(1)}, u32[]{:S(2)}, u32[]{:S(2)}) collective-permute-start(f32[4,32,256]{2,1,0:T(8,128)S(1)} %fusion), channel_id=1, source_target_pairs={{0,16},{8,24},{16,0},{24,8},{1,17},{9,25},{17,1},{25,9},{2,18},{10... | collective-permute-start | bytes 393224 | tf_op jit(solution)/shard_map/ppermute | solution.py:18
  172.2 7.3 %collective-permute-start.6 = (f32[4,32,256]{2,1,0:T(8,128)S(1)}, f32[4,32,256]{2,1,0:T(8,128)S(1)}, u32[]{:S(2)}, u32[]{:S(2)}) collective-permute-start(f32[4,32,256]{2,1,0:T(8,128)S(1)} %fusion), channel_id=1, source_target_pairs={{0,24},{8,16},{16,8},{24,0},{1,25},{9,17},{17,9},{25,1},{2,26},{10... | collective-permute-start | bytes 393224 | tf_op jit(solution)/shard_map/ppermute | solution.py:18
  175.0 6.1 %collective-permute-start.4 = (f32[4,32,256]{2,1,0:T(8,128)S(1)}, f32[4,32,256]{2,1,0:T(8,128)S(1)}, u32[]{:S(2)}, u32[]{:S(2)}) collective-permute-start(f32[4,32,256]{2,1,0:T(8,128)S(1)} %fusion), channel_id=1, source_target_pairs={{0,8},{8,0},{16,24},{24,16},{1,9},{9,1},{17,25},{25,17},{2,10},{10... | collective-permute-start | bytes 393224 | tf_op jit(solution)/shard_map/ppermute | solution.py:18
  181.2 16.2 %collective-permute-start.7 = (f32[32,256]{1,0:T(8,128)S(1)}, f32[32,256]{1,0:T(8,128)S(1)}, u32[]{:S(2)}, u32[]{:S(2)}) collective-permute-start(f32[32,256]{1,0:T(8,128)S(1)} %get-tuple-element.23), channel_id=1, source_target_pairs={{0,128},{128,0},{256,384},{384,256},{1,129},{129,1},{257,385},{385... | collective-permute-start | bytes 98312 | tf_op jit(solution)/shard_map/ppermute | solution.py:18
  188.3 13.4 %collective-permute-start.8 = (f32[32,256]{1,0:T(8,128)S(1)}, f32[32,256]{1,0:T(8,128)S(1)}, u32[]{:S(2)}, u32[]{:S(2)}) collective-permute-start(f32[32,256]{1,0:T(8,128)S(1)} %get-tuple-element.22), channel_id=1, source_target_pairs={{0,256},{128,384},{256,0},{384,128},{1,257},{129,385},{257,1},{385... | collective-permute-start | bytes 98312 | tf_op jit(solution)/shard_map/ppermute | solution.py:18
  195.2 9.2 %collective-permute-start.9 = (f32[32,256]{1,0:T(8,128)S(1)}, f32[32,256]{1,0:T(8,128)S(1)}, u32[]{:S(2)}, u32[]{:S(2)}) collective-permute-start(f32[32,256]{1,0:T(8,128)S(1)} %get-tuple-element.21), channel_id=1, source_target_pairs={{0,384},{128,256},{256,128},{384,0},{1,385},{129,257},{257,129},{3... | collective-permute-start | bytes 98312 | tf_op jit(solution)/shard_map/ppermute | solution.py:18
  204.4 5.7 %collective-permute-start.10 = (f32[32,256]{1,0:T(8,128)S(1)}, f32[32,256]{1,0:T(8,128)S(1)}, u32[]{:S(2)}, u32[]{:S(2)}) collective-permute-start(f32[32,256]{1,0:T(8,128)S(1)} %fusion.1), channel_id=1, source_target_pairs={{0,2},{2,0},{4,6},{6,4},{1,3},{3,1},{5,7},{7,5},{8,10},{10,8},{12,... | collective-permute-start | bytes 98312 | tf_op jit(solution)/shard_map/ppermute | solution.py:18
  210.1 6.2 %collective-permute-start.11 = (f32[32,256]{1,0:T(8,128)S(1)}, f32[32,256]{1,0:T(8,128)S(1)}, u32[]{:S(2)}, u32[]{:S(2)}) collective-permute-start(f32[32,256]{1,0:T(8,128)S(1)} %add.110), channel_id=1, source_target_pairs={{0,4},{2,6},{4,0},{6,2},{1,5},{3,7},{5,1},{7,3},{8,12},{10,14},{12... | collective-permute-start | bytes 98312 | tf_op jit(solution)/shard_map/ppermute | solution.py:18
  216.4 8.6 %collective-permute-start.12 = (f32[32,256]{1,0:T(8,128)S(1)}, f32[32,256]{1,0:T(8,128)S(1)}, u32[]{:S(2)}, u32[]{:S(2)}) collective-permute-start(f32[32,256]{1,0:T(8,128)S(1)} %add.111), channel_id=1, source_target_pairs={{0,1},{1,0},{2,3},{3,2},{4,5},{5,4},{6,7},{7,6},{8,9},{9,8},{10,11... | collective-permute-start | bytes 98312 | tf_op jit(solution)/shard_map/ppermute | solution.py:18

commit v4 on v3

--- a/solution.py
+++ b/solution.py
@@ -63,12 +63,11 @@
     own = lax.dynamic_slice_in_dim(partial_gram, core * half, half, 1)
     terms = (own + swap(other, "core", 1)).reshape(4, 4, order // 16, half)
     terms = scatter_sum(terms.transpose(1, 0, 2, 3), "y")
-    terms = sum_swapped([terms] * 4, "x")
+    terms = lax.all_gather(terms, "x").sum(0)
     rows = scatter_sum(terms, "zh")
     rows = rows + swap(rows, "zl", 1)
     rows = rows + swap(rows, "zl", 2)
-    beside = swap(rows, "core", 1)
-    return jnp.concatenate([jnp.where(core == 0, rows, beside), jnp.where(core == 0, beside, rows)], axis=1)
+    return lax.all_gather(rows, "core", axis=1, tiled=True)
 
 
 def dot(a, b):

time: 229 us -> 226 us (0.987)
  blocking collectives: 23.7 us -> 43.3 us
  starting transfers between devices: 91.2 us -> 73.7 us
  waiting for transfers between devices: 100 us -> 94.7 us
    all_gather x0 -> x2, blocking collectives: none -> 19.6 us  [the longest x1 12.2 us: reduce_gram(): terms = lax.all_gather(terms, 'x').sum(0)]
    ppermute x17 -> x13, starting transfers between devices: 70.1 us -> 52.6 us  [swap(): return lax.ppermute(value, axis, [(i, i ^ flip) for i in range(count)])]
    ppermute x17 -> x13, waiting for transfers between devices: 33.9 us -> 28.6 us  [swap(): return lax.ppermute(value, axis, [(i, i ^ flip) for i in range(count)])]
  transfers between devices with their start and end apart: 19 -> 15, of which waited for: 15 -> 12; matrix products, arithmetic and copies ran while one was open for 1% -> 1% of each run, Pallas kernels for 0% -> 0%
where the time goes in v4:
time: 226 us; the launch traced here: 225 us
  waiting for transfers between devices  94.7 us (42%)
  starting transfers between devices  73.7 us (33%)
  blocking collectives  43.3 us (19%)
  local copies, waits for them, and re-layouts  8.47 us (4%)
  matrix products  3.9 us (2%)
    all_to_all x2, waiting for transfers between devices, exchange(): return lax.all_to_all(value, axis, split_axis=0, concat_axis=0, tiled=True)  66.1 us
    ppermute x13, starting transfers between devices, swap(): return lax.ppermute(value, axis, [(i, i ^ flip) for i in range(count)])  52.6 us
    ppermute x13, waiting for transfers between devices, swap(): return lax.ppermute(value, axis, [(i, i ^ flip) for i in range(count)])  28.6 us
    all_gather x1, blocking collectives, gather_zh(): return lax.all_gather(part, 'zh')  23.7 us
    all_to_all x2, starting transfers between devices, exchange(): return lax.all_to_all(value, axis, split_axis=0, concat_axis=0, tiled=True)  21.1 us
    all_gather x1, blocking collectives, reduce_gram(): terms = lax.all_gather(terms, 'x').sum(0)  12.2 us
    all_gather x1, blocking collectives, reduce_gram(): return lax.all_gather(rows, 'core', axis=1, tiled=True)  7.41 us
  transfers between devices with their start and end apart: 15, of which 12 were waited for; matrix products, arithmetic and copies ran while one was open for 1% of the time, Pallas kernels for 0%

profile of v4, /device:TPU:1, one launch (start us, length us, event | category | flops | bytes accessed | tf_op | source)
XLA Modules:
  0.0 225.3 jit_solution(1237258575235899268)
XLA Ops:
  0.6 0.0 copy-start
  0.6 1.9 reshape.29
  2.6 2.5 %copy.21 = f32[32,16,1024]{2,0,1:T(8,128)} copy(f32[32,16,1024]{2,1,0:T(8,128)S(1)} %reshape.29) | data formatting | bytes 4194304 | tf_op jit(solution)/shard_map/reshape | solution.py:79
  5.1 0.0 copy-done
  5.1 23.7 %all-gather = f32[32,256]{1,0:T(8,128)S(1)} all-gather(f32[8,256]{1,0:T(8,128)S(1)} %constant_dynamic-slice_fusion.9), channel_id=2, replica_groups=mesh['zh'=4,'y'=4,'x'=4,'zl'=4,'core'=2] {'zh'}, dimensions={0}, use_global_device_ids=true | all-gather | bytes 40960 | tf_op jit(solution)/shard_map/all_gather | solution.py:50
  28.8 9.1 %all-to-all-start = ((f32[16,32,1024]{2,1,0:T(8,128)}), f32[16,32,1024]{2,1,0:T(8,128)S(1)}, u32[]{:S(2)}, u32[]{:S(2)}) async-start(f32[16,32,1024]{2,1,0:T(8,128)} %bitcast.53), calls=%async_computation | async-start | bytes 4194304 | tf_op jit(solution)/shard_map/all_to_all | solution.py:13
  37.9 3.3 %collective-permute-start.9 = (f32[4,8,256]{2,1,0:T(8,128)S(1)}, f32[4,8,256]{2,1,0:T(8,128)S(1)}, u32[]{:S(2)}, u32[]{:S(2)}) collective-permute-start(f32[4,8,256]{2,1,0:T(8,128)S(1)} %bitcast.61), channel_id=1, source_target_pairs={{0,32},{32,0},{64,96},{96,64},{1,33},{33,1},{65,97},{97,65},{2,34}... | collective-permute-start | bytes 98312 | tf_op jit(solution)/shard_map/ppermute | solution.py:18
  41.2 2.4 %collective-permute-done.9 = f32[4,8,256]{2,1,0:T(8,128)S(1)} collective-permute-done((f32[4,8,256]{2,1,0:T(8,128)S(1)}, f32[4,8,256]{2,1,0:T(8,128)S(1)}, u32[]{:S(2)}, u32[]{:S(2)}) %collective-permute-start.9) | collective-permute-done | bytes 32800 | tf_op jit(solution)/shard_map/ppermute | solution.py:18
  43.6 3.7 %collective-permute-start.10 = (f32[2,4,8,256]{3,2,0,1:T(8,128)S(1)}, f32[2,4,8,256]{3,2,0,1:T(8,128)S(1)}, u32[]{:S(2)}, u32[]{:S(2)}) collective-permute-start(f32[2,4,8,256]{3,2,0,1:T(8,128)S(1)} %pad_maximum_fusion.5), channel_id=1, source_target_pairs={{0,96},{32,64},{64,32},{96,0},{1,97},{33,65},{65,33},{97,1},{2,98}... | collective-permute-start | bytes 196616 | tf_op jit(solution)/shard_map/ppermute | solution.py:18
  47.4 3.0 %collective-permute-done.10 = f32[2,4,8,256]{3,2,0,1:T(8,128)S(1)} collective-permute-done((f32[2,4,8,256]{3,2,0,1:T(8,128)S(1)}, f32[2,4,8,256]{3,2,0,1:T(8,128)S(1)}, u32[]{:S(2)}, u32[]{:S(2)}) %collective-permute-start.10) | collective-permute-done | bytes 65568 | tf_op jit(solution)/shard_map/ppermute | solution.py:18
  50.4 3.1 %collective-permute-start.11 = (f32[4,4,8,256]{3,2,0,1:T(8,128)S(1)}, f32[4,4,8,256]{3,2,0,1:T(8,128)S(1)}, u32[]{:S(2)}, u32[]{:S(2)}) collective-permute-start(f32[4,4,8,256]{3,2,0,1:T(8,128)S(1)} %get-tuple-element.16), channel_id=1, source_target_pairs={{0,8},{8,0},{16,24},{24,16},{1,9},{9,1},{17,25},{25,17},{2,10},{10... | collective-permute-start | bytes 393224 | tf_op jit(solution)/shard_map/ppermute | solution.py:18
  53.5 2.9 %collective-permute-done.11 = f32[4,4,8,256]{3,2,0,1:T(8,128)S(1)} collective-permute-done((f32[4,4,8,256]{3,2,0,1:T(8,128)S(1)}, f32[4,4,8,256]{3,2,0,1:T(8,128)S(1)}, u32[]{:S(2)}, u32[]{:S(2)}) %collective-permute-start.11) | collective-permute-done | bytes 131104 | tf_op jit(solution)/shard_map/ppermute | solution.py:18
  56.4 4.4 %collective-permute-start.12 = (f32[2,4,4,8,256]{4,3,0,1,2:T(8,128)S(1)}, f32[2,4,4,8,256]{4,3,0,1,2:T(8,128)S(1)}, u32[]{:S(2)}, u32[]{:S(2)}) collective-permute-start(f32[2,4,4,8,256]{4,3,0,1,2:T(8,128)S(1)} %pad_maximum_fusion.2), channel_id=1, source_target_pairs={{0,24},{8,16},{16,8},{24,0},{1,25},{9,17},{17,9},{25,1},{2,26},{10... | collective-permute-start | bytes 786440 | tf_op jit(solution)/shard_map/ppermute | solution.py:18
  60.8 4.2 %collective-permute-done.12 = f32[2,4,4,8,256]{4,3,0,1,2:T(8,128)S(1)} collective-permute-done((f32[2,4,4,8,256]{4,3,0,1,2:T(8,128)S(1)}, f32[2,4,4,8,256]{4,3,0,1,2:T(8,128)S(1)}, u32[]{:S(2)}, u32[]{:S(2)}) %collective-permute-start.12) | collective-permute-done | bytes 262176 | tf_op jit(solution)/shard_map/ppermute | solution.py:18
  65.2 0.2 copy.18
  65.4 66.1 %all-to-all-done = f32[16,32,1024]{2,1,0:T(8,128)S(1)} async-done(((f32[16,32,1024]{2,1,0:T(8,128)}), f32[16,32,1024]{2,1,0:T(8,128)S(1)}, u32[]{:S(2)}, u32[]{:S(2)}) %all-to-all-start) | async-done | bytes 2097184 | tf_op jit(solution)/shard_map/all_to_all | solution.py:13
  131.5 2.1 fusion.6
  133.6 12.0 %all-to-all-start.1 = ((f32[16,16,1024]{2,1,0:T(8,128)}), f32[16,16,1024]{2,1,0:T(8,128)}, u32[]{:S(2)}, u32[]{:S(2)}) async-start(f32[16,16,1024]{2,1,0:T(8,128)} %fusion.6), calls=%async_computation.1 | async-start | bytes 2097152 | tf_op jit(solution)/shard_map/all_to_all | solution.py:13
  145.6 1.8 fusion.5
  147.5 3.2 %collective-permute-start = (f32[512,256]{1,0:T(8,128)S(1)}, f32[512,256]{1,0:T(8,128)S(1)}, u32[]{:S(2)}, u32[]{:S(2)}) collective-permute-start(f32[512,256]{1,0:T(8,128)S(1)} %constant_dynamic-slice_fusion.8), channel_id=1, source_target_pairs={{0,1},{1,0},{2,3},{3,2},{4,5},{5,4},{6,7},{7,6},{8,9},{9,8},{10,11... | collective-permute-start | bytes 1572872 | tf_op jit(solution)/shard_map/ppermute | solution.py:18
  150.7 1.5 collective-permute-done
  152.2 0.1 dynamic-slice_add_fusion
  152.4 3.5 %collective-permute-start.1 = (f32[4,32,256]{2,1,0:T(8,128)S(1)}, f32[4,32,256]{2,1,0:T(8,128)S(1)}, u32[]{:S(2)}, u32[]{:S(2)}) collective-permute-start(f32[4,32,256]{2,1,0:T(8,128)S(1)} %get-tuple-element.12), channel_id=1, source_target_pairs={{0,32},{32,0},{64,96},{96,64},{1,33},{33,1},{65,97},{97,65},{2,34}... | collective-permute-start | bytes 393224 | tf_op jit(solution)/shard_map/ppermute | solution.py:18
  155.9 4.3 %collective-permute-start.2 = (f32[4,32,256]{2,1,0:T(8,128)S(1)}, f32[4,32,256]{2,1,0:T(8,128)S(1)}, u32[]{:S(2)}, u32[]{:S(2)}) collective-permute-start(f32[4,32,256]{2,1,0:T(8,128)S(1)} %get-tuple-element.11), channel_id=1, source_target_pairs={{0,64},{32,96},{64,0},{96,32},{1,65},{33,97},{65,1},{97,33},{2,66}... | collective-permute-start | bytes 393224 | tf_op jit(solution)/shard_map/ppermute | solution.py:18
  160.2 1.9 collective-permute-start.3
  162.2 0.0 collective-permute-done.1
  162.2 3.0 %collective-permute-done.2 = f32[4,32,256]{2,1,0:T(8,128)S(1)} collective-permute-done((f32[4,32,256]{2,1,0:T(8,128)S(1)}, f32[4,32,256]{2,1,0:T(8,128)S(1)}, u32[]{:S(2)}, u32[]{:S(2)}) %collective-permute-start.2) | collective-permute-done | bytes 131104 | tf_op jit(solution)/shard_map/ppermute | solution.py:18
  165.1 2.4 %collective-permute-done.3 = f32[4,32,256]{2,1,0:T(8,128)S(1)} collective-permute-done((f32[4,32,256]{2,1,0:T(8,128)S(1)}, f32[4,32,256]{2,1,0:T(8,128)S(1)}, u32[]{:S(2)}, u32[]{:S(2)}) %collective-permute-start.3) | collective-permute-done | bytes 131104 | tf_op jit(solution)/shard_map/ppermute | solution.py:18
  167.6 12.2 %all-gather.1 = f32[16,32,256]{2,1,0:T(8,128)S(1)} all-gather(f32[4,32,256]{2,1,0:T(8,128)S(1)} %fusion), channel_id=3, replica_groups=mesh['zh'=4,'y'=4,'x'=4,'zl'=4,'core'=2] {'x'}, dimensions={0}, use_global_device_ids=true | all-gather | bytes 655360 | tf_op jit(solution)/shard_map/all_gather | solution.py:66
  179.8 7.1 %collective-permute-start.4 = (f32[32,256]{1,0:T(8,128)S(1)}, f32[32,256]{1,0:T(8,128)S(1)}, u32[]{:S(2)}, u32[]{:S(2)}) collective-permute-start(f32[32,256]{1,0:T(8,128)S(1)} %get-tuple-element.23), channel_id=1, source_target_pairs={{0,128},{128,0},{256,384},{384,256},{1,129},{129,1},{257,385},{385... | collective-permute-start | bytes 98312 | tf_op jit(solution)/shard_map/ppermute | solution.py:18
  186.9 7.0 %collective-permute-start.5 = (f32[32,256]{1,0:T(8,128)S(1)}, f32[32,256]{1,0:T(8,128)S(1)}, u32[]{:S(2)}, u32[]{:S(2)}) collective-permute-start(f32[32,256]{1,0:T(8,128)S(1)} %get-tuple-element.22), channel_id=1, source_target_pairs={{0,256},{128,384},{256,0},{384,128},{1,257},{129,385},{257,1},{385... | collective-permute-start | bytes 98312 | tf_op jit(solution)/shard_map/ppermute | solution.py:18
  193.8 2.2 collective-permute-start.6
  196.0 0.0 collective-permute-done.4
  196.0 4.2 %collective-permute-done.5 = f32[32,256]{1,0:T(8,128)S(1)} collective-permute-done((f32[32,256]{1,0:T(8,128)S(1)}, f32[32,256]{1,0:T(8,128)S(1)}, u32[]{:S(2)}, u32[]{:S(2)}) %collective-permute-start.5) | collective-permute-done | bytes 32800 | tf_op jit(solution)/shard_map/ppermute | solution.py:18
  200.3 2.4 %collective-permute-done.6 = f32[32,256]{1,0:T(8,128)S(1)} collective-permute-done((f32[32,256]{1,0:T(8,128)S(1)}, f32[32,256]{1,0:T(8,128)S(1)}, u32[]{:S(2)}, u32[]{:S(2)}) %collective-permute-start.6) | collective-permute-done | bytes 32800 | tf_op jit(solution)/shard_map/ppermute | solution.py:18
  202.7 3.8 %collective-permute-start.7 = (f32[32,256]{1,0:T(8,128)S(1)}, f32[32,256]{1,0:T(8,128)S(1)}, u32[]{:S(2)}, u32[]{:S(2)}) collective-permute-start(f32[32,256]{1,0:T(8,128)S(1)} %fusion.1), channel_id=1, source_target_pairs={{0,2},{2,0},{4,6},{6,4},{1,3},{3,1},{5,7},{7,5},{8,10},{10,8},{12,... | collective-permute-start | bytes 98312 | tf_op jit(solution)/shard_map/ppermute | solution.py:18
  206.5 1.3 collective-permute-done.7
  207.8 5.1 %collective-permute-start.8 = (f32[32,256]{1,0:T(8,128)S(1)}, f32[32,256]{1,0:T(8,128)S(1)}, u32[]{:S(2)}, u32[]{:S(2)}) collective-permute-start(f32[32,256]{1,0:T(8,128)S(1)} %add.98), channel_id=1, source_target_pairs={{0,4},{2,6},{4,0},{6,2},{1,5},{3,7},{5,1},{7,3},{8,12},{10,14},{12... | collective-permute-start | bytes 98312 | tf_op jit(solution)/shard_map/ppermute | solution.py:18
  213.0 1.3 collective-permute-done.8
  214.3 7.4 %all_gather.19 = f32[32,512]{1,0:T(8,128)S(1)} all-gather(f32[32,256]{1,0:T(8,128)S(1)} %add.99), channel_id=1, replica_groups=mesh['zh'=4,'y'=4,'x'=4,'zl'=4,'core'=2] {'core'}, dimensions={1}, use_global_device_ids=true | all-gather | bytes 98304 | tf_op jit(solution)/shard_map/all_gather | solution.py:70
  221.7 0.0 all-to-all-done.1
  221.7 1.8 copy.19
  223.5 1.1 reshape.33
  224.7 0.6 copy.23
  (19 shorter events, 0.4 us)
Async XLA Ops:
  0.6 4.5 %copy-start = (f32[32,256]{1,0:T(8,128)S(1)}, f32[32,256]{1,0:T(8,128)}, u32[]{:S(2)}) copy-start(f32[32,256]{1,0:T(8,128)} %param.3) | copy-start | bytes 98308
  28.8 102.7 %all-to-all-start = ((f32[16,32,1024]{2,1,0:T(8,128)}), f32[16,32,1024]{2,1,0:T(8,128)S(1)}, u32[]{:S(2)}, u32[]{:S(2)}) async-start(f32[16,32,1024]{2,1,0:T(8,128)} %bitcast.53), calls=%async_computation | async-start | bytes 4194304 | tf_op jit(solution)/shard_map/all_to_all | solution.py:13
  37.9 5.7 %collective-permute-start.9 = (f32[4,8,256]{2,1,0:T(8,128)S(1)}, f32[4,8,256]{2,1,0:T(8,128)S(1)}, u32[]{:S(2)}, u32[]{:S(2)}) collective-permute-start(f32[4,8,256]{2,1,0:T(8,128)S(1)} %bitcast.61), channel_id=1, source_target_pairs={{0,32},{32,0},{64,96},{96,64},{1,33},{33,1},{65,97},{97,65},{2,34}... | collective-permute-start | bytes 98312 | tf_op jit(solution)/shard_map/ppermute | solution.py:18
  43.6 6.7 %collective-permute-start.10 = (f32[2,4,8,256]{3,2,0,1:T(8,128)S(1)}, f32[2,4,8,256]{3,2,0,1:T(8,128)S(1)}, u32[]{:S(2)}, u32[]{:S(2)}) collective-permute-start(f32[2,4,8,256]{3,2,0,1:T(8,128)S(1)} %pad_maximum_fusion.5), channel_id=1, source_target_pairs={{0,96},{32,64},{64,32},{96,0},{1,97},{33,65},{65,33},{97,1},{2,98}... | collective-permute-start | bytes 196616 | tf_op jit(solution)/shard_map/ppermute | solution.py:18
  50.4 6.0 %collective-permute-start.11 = (f32[4,4,8,256]{3,2,0,1:T(8,128)S(1)}, f32[4,4,8,256]{3,2,0,1:T(8,128)S(1)}, u32[]{:S(2)}, u32[]{:S(2)}) collective-permute-start(f32[4,4,8,256]{3,2,0,1:T(8,128)S(1)} %get-tuple-element.16), channel_id=1, source_target_pairs={{0,8},{8,0},{16,24},{24,16},{1,9},{9,1},{17,25},{25,17},{2,10},{10... | collective-permute-start | bytes 393224 | tf_op jit(solution)/shard_map/ppermute | solution.py:18
  56.4 8.6 %collective-permute-start.12 = (f32[2,4,4,8,256]{4,3,0,1,2:T(8,128)S(1)}, f32[2,4,4,8,256]{4,3,0,1,2:T(8,128)S(1)}, u32[]{:S(2)}, u32[]{:S(2)}) collective-permute-start(f32[2,4,4,8,256]{4,3,0,1,2:T(8,128)S(1)} %pad_maximum_fusion.2), channel_id=1, source_target_pairs={{0,24},{8,16},{16,8},{24,0},{1,25},{9,17},{17,9},{25,1},{2,26},{10... | collective-permute-start | bytes 786440 | tf_op jit(solution)/shard_map/ppermute | solution.py:18
  133.6 88.1 %all-to-all-start.1 = ((f32[16,16,1024]{2,1,0:T(8,128)}), f32[16,16,1024]{2,1,0:T(8,128)}, u32[]{:S(2)}, u32[]{:S(2)}) async-start(f32[16,16,1024]{2,1,0:T(8,128)} %fusion.6), calls=%async_computation.1 | async-start | bytes 2097152 | tf_op jit(solution)/shard_map/all_to_all | solution.py:13
  147.5 4.8 %collective-permute-start = (f32[512,256]{1,0:T(8,128)S(1)}, f32[512,256]{1,0:T(8,128)S(1)}, u32[]{:S(2)}, u32[]{:S(2)}) collective-permute-start(f32[512,256]{1,0:T(8,128)S(1)} %constant_dynamic-slice_fusion.8), channel_id=1, source_target_pairs={{0,1},{1,0},{2,3},{3,2},{4,5},{5,4},{6,7},{7,6},{8,9},{9,8},{10,11... | collective-permute-start | bytes 1572872 | tf_op jit(solution)/shard_map/ppermute | solution.py:18
  152.4 9.8 %collective-permute-start.1 = (f32[4,32,256]{2,1,0:T(8,128)S(1)}, f32[4,32,256]{2,1,0:T(8,128)S(1)}, u32[]{:S(2)}, u32[]{:S(2)}) collective-permute-start(f32[4,32,256]{2,1,0:T(8,128)S(1)} %get-tuple-element.12), channel_id=1, source_target_pairs={{0,32},{32,0},{64,96},{96,64},{1,33},{33,1},{65,97},{97,65},{2,34}... | collective-permute-start | bytes 393224 | tf_op jit(solution)/shard_map/ppermute | solution.py:18
  155.9 9.2 %collective-permute-start.2 = (f32[4,32,256]{2,1,0:T(8,128)S(1)}, f32[4,32,256]{2,1,0:T(8,128)S(1)}, u32[]{:S(2)}, u32[]{:S(2)}) collective-permute-start(f32[4,32,256]{2,1,0:T(8,128)S(1)} %get-tuple-element.11), channel_id=1, source_target_pairs={{0,64},{32,96},{64,0},{96,32},{1,65},{33,97},{65,1},{97,33},{2,66}... | collective-permute-start | bytes 393224 | tf_op jit(solution)/shard_map/ppermute | solution.py:18
  160.2 7.3 %collective-permute-start.3 = (f32[4,32,256]{2,1,0:T(8,128)S(1)}, f32[4,32,256]{2,1,0:T(8,128)S(1)}, u32[]{:S(2)}, u32[]{:S(2)}) collective-permute-start(f32[4,32,256]{2,1,0:T(8,128)S(1)} %get-tuple-element.10), channel_id=1, source_target_pairs={{0,96},{32,64},{64,32},{96,0},{1,97},{33,65},{65,33},{97,1},{2,98}... | collective-permute-start | bytes 393224 | tf_op jit(solution)/shard_map/ppermute | solution.py:18
  179.8 16.2 %collective-permute-start.4 = (f32[32,256]{1,0:T(8,128)S(1)}, f32[32,256]{1,0:T(8,128)S(1)}, u32[]{:S(2)}, u32[]{:S(2)}) collective-permute-start(f32[32,256]{1,0:T(8,128)S(1)} %get-tuple-element.23), channel_id=1, source_target_pairs={{0,128},{128,0},{256,384},{384,256},{1,129},{129,1},{257,385},{385... | collective-permute-start | bytes 98312 | tf_op jit(solution)/shard_map/ppermute | solution.py:18
  186.9 13.4 %collective-permute-start.5 = (f32[32,256]{1,0:T(8,128)S(1)}, f32[32,256]{1,0:T(8,128)S(1)}, u32[]{:S(2)}, u32[]{:S(2)}) collective-permute-start(f32[32,256]{1,0:T(8,128)S(1)} %get-tuple-element.22), channel_id=1, source_target_pairs={{0,256},{128,384},{256,0},{384,128},{1,257},{129,385},{257,1},{385... | collective-permute-start | bytes 98312 | tf_op jit(solution)/shard_map/ppermute | solution.py:18
  193.8 8.9 %collective-permute-start.6 = (f32[32,256]{1,0:T(8,128)S(1)}, f32[32,256]{1,0:T(8,128)S(1)}, u32[]{:S(2)}, u32[]{:S(2)}) collective-permute-start(f32[32,256]{1,0:T(8,128)S(1)} %get-tuple-element.21), channel_id=1, source_target_pairs={{0,384},{128,256},{256,128},{384,0},{1,385},{129,257},{257,129},{3... | collective-permute-start | bytes 98312 | tf_op jit(solution)/shard_map/ppermute | solution.py:18
  202.7 5.1 %collective-permute-start.7 = (f32[32,256]{1,0:T(8,128)S(1)}, f32[32,256]{1,0:T(8,128)S(1)}, u32[]{:S(2)}, u32[]{:S(2)}) collective-permute-start(f32[32,256]{1,0:T(8,128)S(1)} %fusion.1), channel_id=1, source_target_pairs={{0,2},{2,0},{4,6},{6,4},{1,3},{3,1},{5,7},{7,5},{8,10},{10,8},{12,... | collective-permute-start | bytes 98312 | tf_op jit(solution)/shard_map/ppermute | solution.py:18
  207.8 6.5 %collective-permute-start.8 = (f32[32,256]{1,0:T(8,128)S(1)}, f32[32,256]{1,0:T(8,128)S(1)}, u32[]{:S(2)}, u32[]{:S(2)}) collective-permute-start(f32[32,256]{1,0:T(8,128)S(1)} %add.98), channel_id=1, source_target_pairs={{0,4},{2,6},{4,0},{6,2},{1,5},{3,7},{5,1},{7,3},{8,12},{10,14},{12... | collective-permute-start | bytes 98312 | tf_op jit(solution)/shard_map/ppermute | solution.py:18

commit v5 on v4

--- a/solution.py
+++ b/solution.py
@@ -65,9 +65,8 @@
     terms = scatter_sum(terms.transpose(1, 0, 2, 3), "y")
     terms = lax.all_gather(terms, "x").sum(0)
     rows = scatter_sum(terms, "zh")
-    rows = rows + swap(rows, "zl", 1)
-    rows = rows + swap(rows, "zl", 2)
-    return lax.all_gather(rows, "core", axis=1, tiled=True)
+    shares = lax.all_gather(rows, ("zl", "core")).reshape(4, 2, *rows.shape).sum(0)
+    return shares.transpose(1, 0, 2).reshape(rows.shape[0], order)
 
 
 def dot(a, b):

time: 226 us -> 227 us (level)
  blocking collectives: 43.3 us -> 55.4 us
  starting transfers between devices: 73.7 us -> 64.7 us
  waiting for transfers between devices: 94.7 us -> 92.1 us
    all_gather x1, blocking collectives: 7.41 us -> 19.5 us  [reduce_gram(): lax.all_gather(rows, ('zl', 'core')).reshape(4, 2, *rows.shape).sum(0)]
    ppermute x13 -> x11, starting transfers between devices: 52.6 us -> 43.6 us  [swap(): return lax.ppermute(value, axis, [(i, i ^ flip) for i in range(count)])]
    ppermute x13 -> x11, waiting for transfers between devices: 28.6 us -> 26 us  [swap(): return lax.ppermute(value, axis, [(i, i ^ flip) for i in range(count)])]
  transfers between devices with their start and end apart: 15 -> 13, of which waited for: 12 -> 10; matrix products, arithmetic and copies ran while one was open for 1% -> 1% of each run, Pallas kernels for 0% -> 0%
where the time goes in v5:
time: 227 us; the launch traced here: 226 us
  waiting for transfers between devices  92.1 us (41%)
  starting transfers between devices  64.7 us (29%)
  blocking collectives  55.4 us (24%)
  local copies, waits for them, and re-layouts  8.49 us (4%)
  matrix products  3.9 us (2%)
    all_to_all x2, waiting for transfers between devices, exchange(): return lax.all_to_all(value, axis, split_axis=0, concat_axis=0, tiled=True)  66.1 us
    ppermute x11, starting transfers between devices, swap(): return lax.ppermute(value, axis, [(i, i ^ flip) for i in range(count)])  43.6 us
    ppermute x11, waiting for transfers between devices, swap(): return lax.ppermute(value, axis, [(i, i ^ flip) for i in range(count)])  26 us
    all_gather x1, blocking collectives, gather_zh(): return lax.all_gather(part, 'zh')  23.7 us
    all_to_all x2, starting transfers between devices, exchange(): return lax.all_to_all(value, axis, split_axis=0, concat_axis=0, tiled=True)  21.1 us
    all_gather x1, blocking collectives, reduce_gram(): lax.all_gather(rows, ('zl', 'core')).reshape(4, 2, *rows.shape).sum(0)  19.5 us
    all_gather x1, blocking collectives, reduce_gram(): terms = lax.all_gather(terms, 'x').sum(0)  12.2 us
  transfers between devices with their start and end apart: 13, of which 10 were waited for; matrix products, arithmetic and copies ran while one was open for 1% of the time, Pallas kernels for 0%

profile of v5, /device:TPU:1, one launch (start us, length us, event | category | flops | bytes accessed | tf_op | source)
XLA Modules:
  0.0 225.9 jit_solution(7900973022911295315)
XLA Ops:
  0.6 0.0 copy-start
  0.6 1.9 reshape.35
  2.6 2.6 %copy.37 = f32[32,16,1024]{2,0,1:T(8,128)} copy(f32[32,16,1024]{2,1,0:T(8,128)S(1)} %reshape.35) | data formatting | bytes 4194304 | tf_op jit(solution)/shard_map/reshape | solution.py:78
  5.2 0.0 copy-done
  5.2 23.7 %all-gather = f32[32,256]{1,0:T(8,128)S(1)} all-gather(f32[8,256]{1,0:T(8,128)S(1)} %constant_dynamic-slice_fusion.9), channel_id=2, replica_groups=mesh['zh'=4,'y'=4,'x'=4,'zl'=4,'core'=2] {'zh'}, dimensions={0}, use_global_device_ids=true | all-gather | bytes 40960 | tf_op jit(solution)/shard_map/all_gather | solution.py:50
  28.8 9.1 %all-to-all-start = ((f32[16,32,1024]{2,1,0:T(8,128)}), f32[16,32,1024]{2,1,0:T(8,128)S(1)}, u32[]{:S(2)}, u32[]{:S(2)}) async-start(f32[16,32,1024]{2,1,0:T(8,128)} %bitcast.57), calls=%async_computation | async-start | bytes 4194304 | tf_op jit(solution)/shard_map/all_to_all | solution.py:13
  37.9 3.3 %collective-permute-start.7 = (f32[4,8,256]{2,1,0:T(8,128)S(1)}, f32[4,8,256]{2,1,0:T(8,128)S(1)}, u32[]{:S(2)}, u32[]{:S(2)}) collective-permute-start(f32[4,8,256]{2,1,0:T(8,128)S(1)} %bitcast.66), channel_id=1, source_target_pairs={{0,32},{32,0},{64,96},{96,64},{1,33},{33,1},{65,97},{97,65},{2,34}... | collective-permute-start | bytes 98312 | tf_op jit(solution)/shard_map/ppermute | solution.py:18
  41.2 2.4 %collective-permute-done.7 = f32[4,8,256]{2,1,0:T(8,128)S(1)} collective-permute-done((f32[4,8,256]{2,1,0:T(8,128)S(1)}, f32[4,8,256]{2,1,0:T(8,128)S(1)}, u32[]{:S(2)}, u32[]{:S(2)}) %collective-permute-start.7) | collective-permute-done | bytes 32800 | tf_op jit(solution)/shard_map/ppermute | solution.py:18
  43.6 3.7 %collective-permute-start.8 = (f32[2,4,8,256]{3,2,0,1:T(8,128)S(1)}, f32[2,4,8,256]{3,2,0,1:T(8,128)S(1)}, u32[]{:S(2)}, u32[]{:S(2)}) collective-permute-start(f32[2,4,8,256]{3,2,0,1:T(8,128)S(1)} %pad_maximum_fusion.5), channel_id=1, source_target_pairs={{0,96},{32,64},{64,32},{96,0},{1,97},{33,65},{65,33},{97,1},{2,98}... | collective-permute-start | bytes 196616 | tf_op jit(solution)/shard_map/ppermute | solution.py:18
  47.4 3.0 %collective-permute-done.8 = f32[2,4,8,256]{3,2,0,1:T(8,128)S(1)} collective-permute-done((f32[2,4,8,256]{3,2,0,1:T(8,128)S(1)}, f32[2,4,8,256]{3,2,0,1:T(8,128)S(1)}, u32[]{:S(2)}, u32[]{:S(2)}) %collective-permute-start.8) | collective-permute-done | bytes 65568 | tf_op jit(solution)/shard_map/ppermute | solution.py:18
  50.4 3.1 %collective-permute-start.9 = (f32[4,4,8,256]{3,2,0,1:T(8,128)S(1)}, f32[4,4,8,256]{3,2,0,1:T(8,128)S(1)}, u32[]{:S(2)}, u32[]{:S(2)}) collective-permute-start(f32[4,4,8,256]{3,2,0,1:T(8,128)S(1)} %get-tuple-element.16), channel_id=1, source_target_pairs={{0,8},{8,0},{16,24},{24,16},{1,9},{9,1},{17,25},{25,17},{2,10},{10... | collective-permute-start | bytes 393224 | tf_op jit(solution)/shard_map/ppermute | solution.py:18
  53.5 2.9 %collective-permute-done.9 = f32[4,4,8,256]{3,2,0,1:T(8,128)S(1)} collective-permute-done((f32[4,4,8,256]{3,2,0,1:T(8,128)S(1)}, f32[4,4,8,256]{3,2,0,1:T(8,128)S(1)}, u32[]{:S(2)}, u32[]{:S(2)}) %collective-permute-start.9) | collective-permute-done | bytes 131104 | tf_op jit(solution)/shard_map/ppermute | solution.py:18
  56.4 4.4 %collective-permute-start.10 = (f32[2,4,4,8,256]{4,3,0,1,2:T(8,128)S(1)}, f32[2,4,4,8,256]{4,3,0,1,2:T(8,128)S(1)}, u32[]{:S(2)}, u32[]{:S(2)}) collective-permute-start(f32[2,4,4,8,256]{4,3,0,1,2:T(8,128)S(1)} %pad_maximum_fusion.2), channel_id=1, source_target_pairs={{0,24},{8,16},{16,8},{24,0},{1,25},{9,17},{17,9},{25,1},{2,26},{10... | collective-permute-start | bytes 786440 | tf_op jit(solution)/shard_map/ppermute | solution.py:18
  60.9 4.2 %collective-permute-done.10 = f32[2,4,4,8,256]{4,3,0,1,2:T(8,128)S(1)} collective-permute-done((f32[2,4,4,8,256]{4,3,0,1,2:T(8,128)S(1)}, f32[2,4,4,8,256]{4,3,0,1,2:T(8,128)S(1)}, u32[]{:S(2)}, u32[]{:S(2)}) %collective-permute-start.10) | collective-permute-done | bytes 262176 | tf_op jit(solution)/shard_map/ppermute | solution.py:18
  65.2 0.2 copy.33
  65.4 66.1 %all-to-all-done = f32[16,32,1024]{2,1,0:T(8,128)S(1)} async-done(((f32[16,32,1024]{2,1,0:T(8,128)}), f32[16,32,1024]{2,1,0:T(8,128)S(1)}, u32[]{:S(2)}, u32[]{:S(2)}) %all-to-all-start) | async-done | bytes 2097184 | tf_op jit(solution)/shard_map/all_to_all | solution.py:13
  131.5 2.1 fusion.6
  133.6 12.0 %all-to-all-start.1 = ((f32[16,16,1024]{2,1,0:T(8,128)}), f32[16,16,1024]{2,1,0:T(8,128)}, u32[]{:S(2)}, u32[]{:S(2)}) async-start(f32[16,16,1024]{2,1,0:T(8,128)} %fusion.6), calls=%async_computation.1 | async-start | bytes 2097152 | tf_op jit(solution)/shard_map/all_to_all | solution.py:13
  145.6 1.8 fusion.5
  147.5 3.2 %collective-permute-start = (f32[512,256]{1,0:T(8,128)S(1)}, f32[512,256]{1,0:T(8,128)S(1)}, u32[]{:S(2)}, u32[]{:S(2)}) collective-permute-start(f32[512,256]{1,0:T(8,128)S(1)} %constant_dynamic-slice_fusion.8), channel_id=1, source_target_pairs={{0,1},{1,0},{2,3},{3,2},{4,5},{5,4},{6,7},{7,6},{8,9},{9,8},{10,11... | collective-permute-start | bytes 1572872 | tf_op jit(solution)/shard_map/ppermute | solution.py:18
  150.7 1.5 collective-permute-done
  152.3 0.1 dynamic-slice_add_fusion
  152.4 3.5 %collective-permute-start.1 = (f32[4,32,256]{2,1,0:T(8,128)S(1)}, f32[4,32,256]{2,1,0:T(8,128)S(1)}, u32[]{:S(2)}, u32[]{:S(2)}) collective-permute-start(f32[4,32,256]{2,1,0:T(8,128)S(1)} %get-tuple-element.12), channel_id=1, source_target_pairs={{0,32},{32,0},{64,96},{96,64},{1,33},{33,1},{65,97},{97,65},{2,34}... | collective-permute-start | bytes 393224 | tf_op jit(solution)/shard_map/ppermute | solution.py:18
  155.9 4.3 %collective-permute-start.2 = (f32[4,32,256]{2,1,0:T(8,128)S(1)}, f32[4,32,256]{2,1,0:T(8,128)S(1)}, u32[]{:S(2)}, u32[]{:S(2)}) collective-permute-start(f32[4,32,256]{2,1,0:T(8,128)S(1)} %get-tuple-element.11), channel_id=1, source_target_pairs={{0,64},{32,96},{64,0},{96,32},{1,65},{33,97},{65,1},{97,33},{2,66}... | collective-permute-start | bytes 393224 | tf_op jit(solution)/shard_map/ppermute | solution.py:18
  160.2 1.9 collective-permute-start.3
  162.2 0.0 collective-permute-done.1
  162.2 3.0 %collective-permute-done.2 = f32[4,32,256]{2,1,0:T(8,128)S(1)} collective-permute-done((f32[4,32,256]{2,1,0:T(8,128)S(1)}, f32[4,32,256]{2,1,0:T(8,128)S(1)}, u32[]{:S(2)}, u32[]{:S(2)}) %collective-permute-start.2) | collective-permute-done | bytes 131104 | tf_op jit(solution)/shard_map/ppermute | solution.py:18
  165.1 2.4 %collective-permute-done.3 = f32[4,32,256]{2,1,0:T(8,128)S(1)} collective-permute-done((f32[4,32,256]{2,1,0:T(8,128)S(1)}, f32[4,32,256]{2,1,0:T(8,128)S(1)}, u32[]{:S(2)}, u32[]{:S(2)}) %collective-permute-start.3) | collective-permute-done | bytes 131104 | tf_op jit(solution)/shard_map/ppermute | solution.py:18
  167.6 12.2 %all-gather.1 = f32[16,32,256]{2,1,0:T(8,128)S(1)} all-gather(f32[4,32,256]{2,1,0:T(8,128)S(1)} %fusion), channel_id=3, replica_groups=mesh['zh'=4,'y'=4,'x'=4,'zl'=4,'core'=2] {'x'}, dimensions={0}, use_global_device_ids=true | all-gather | bytes 655360 | tf_op jit(solution)/shard_map/all_gather | solution.py:66
  179.8 7.1 %collective-permute-start.4 = (f32[32,256]{1,0:T(8,128)S(1)}, f32[32,256]{1,0:T(8,128)S(1)}, u32[]{:S(2)}, u32[]{:S(2)}) collective-permute-start(f32[32,256]{1,0:T(8,128)S(1)} %get-tuple-element.23), channel_id=1, source_target_pairs={{0,128},{128,0},{256,384},{384,256},{1,129},{129,1},{257,385},{385... | collective-permute-start | bytes 98312 | tf_op jit(solution)/shard_map/ppermute | solution.py:18
  186.9 7.0 %collective-permute-start.5 = (f32[32,256]{1,0:T(8,128)S(1)}, f32[32,256]{1,0:T(8,128)S(1)}, u32[]{:S(2)}, u32[]{:S(2)}) collective-permute-start(f32[32,256]{1,0:T(8,128)S(1)} %get-tuple-element.22), channel_id=1, source_target_pairs={{0,256},{128,384},{256,0},{384,128},{1,257},{129,385},{257,1},{385... | collective-permute-start | bytes 98312 | tf_op jit(solution)/shard_map/ppermute | solution.py:18
  193.9 2.2 collective-permute-start.6
  196.0 0.0 collective-permute-done.4
  196.0 4.2 %collective-permute-done.5 = f32[32,256]{1,0:T(8,128)S(1)} collective-permute-done((f32[32,256]{1,0:T(8,128)S(1)}, f32[32,256]{1,0:T(8,128)S(1)}, u32[]{:S(2)}, u32[]{:S(2)}) %collective-permute-start.5) | collective-permute-done | bytes 32800 | tf_op jit(solution)/shard_map/ppermute | solution.py:18
  200.3 2.4 %collective-permute-done.6 = f32[32,256]{1,0:T(8,128)S(1)} collective-permute-done((f32[32,256]{1,0:T(8,128)S(1)}, f32[32,256]{1,0:T(8,128)S(1)}, u32[]{:S(2)}, u32[]{:S(2)}) %collective-permute-start.6) | collective-permute-done | bytes 32800 | tf_op jit(solution)/shard_map/ppermute | solution.py:18
  202.7 19.5 %all-gather.2 = f32[256,256]{1,0:T(8,128)S(1)} all-gather(f32[32,256]{1,0:T(8,128)S(1)} %fusion.1), channel_id=4, replica_groups=mesh['zh'=4,'y'=4,'x'=4,'zl'=4,'core'=2] {'zl','core'}, dimensions={0}, use_global_device_ids=true | all-gather | bytes 294912 | tf_op jit(solution)/shard_map/all_gather | solution.py:68
  222.3 0.6 copy.35
  222.9 0.0 all-to-all-done.1
  222.9 1.8 copy.34
  224.8 1.1 reshape.41
  (18 shorter events, 0.4 us)
Async XLA Ops:
  0.6 4.5 %copy-start = (f32[32,256]{1,0:T(8,128)S(1)}, f32[32,256]{1,0:T(8,128)}, u32[]{:S(2)}) copy-start(f32[32,256]{1,0:T(8,128)} %param.3) | copy-start | bytes 98308
  28.8 102.7 %all-to-all-start = ((f32[16,32,1024]{2,1,0:T(8,128)}), f32[16,32,1024]{2,1,0:T(8,128)S(1)}, u32[]{:S(2)}, u32[]{:S(2)}) async-start(f32[16,32,1024]{2,1,0:T(8,128)} %bitcast.57), calls=%async_computation | async-start | bytes 4194304 | tf_op jit(solution)/shard_map/all_to_all | solution.py:13
  37.9 5.7 %collective-permute-start.7 = (f32[4,8,256]{2,1,0:T(8,128)S(1)}, f32[4,8,256]{2,1,0:T(8,128)S(1)}, u32[]{:S(2)}, u32[]{:S(2)}) collective-permute-start(f32[4,8,256]{2,1,0:T(8,128)S(1)} %bitcast.66), channel_id=1, source_target_pairs={{0,32},{32,0},{64,96},{96,64},{1,33},{33,1},{65,97},{97,65},{2,34}... | collective-permute-start | bytes 98312 | tf_op jit(solution)/shard_map/ppermute | solution.py:18
  43.6 6.7 %collective-permute-start.8 = (f32[2,4,8,256]{3,2,0,1:T(8,128)S(1)}, f32[2,4,8,256]{3,2,0,1:T(8,128)S(1)}, u32[]{:S(2)}, u32[]{:S(2)}) collective-permute-start(f32[2,4,8,256]{3,2,0,1:T(8,128)S(1)} %pad_maximum_fusion.5), channel_id=1, source_target_pairs={{0,96},{32,64},{64,32},{96,0},{1,97},{33,65},{65,33},{97,1},{2,98}... | collective-permute-start | bytes 196616 | tf_op jit(solution)/shard_map/ppermute | solution.py:18
  50.4 6.0 %collective-permute-start.9 = (f32[4,4,8,256]{3,2,0,1:T(8,128)S(1)}, f32[4,4,8,256]{3,2,0,1:T(8,128)S(1)}, u32[]{:S(2)}, u32[]{:S(2)}) collective-permute-start(f32[4,4,8,256]{3,2,0,1:T(8,128)S(1)} %get-tuple-element.16), channel_id=1, source_target_pairs={{0,8},{8,0},{16,24},{24,16},{1,9},{9,1},{17,25},{25,17},{2,10},{10... | collective-permute-start | bytes 393224 | tf_op jit(solution)/shard_map/ppermute | solution.py:18
  56.4 8.6 %collective-permute-start.10 = (f32[2,4,4,8,256]{4,3,0,1,2:T(8,128)S(1)}, f32[2,4,4,8,256]{4,3,0,1,2:T(8,128)S(1)}, u32[]{:S(2)}, u32[]{:S(2)}) collective-permute-start(f32[2,4,4,8,256]{4,3,0,1,2:T(8,128)S(1)} %pad_maximum_fusion.2), channel_id=1, source_target_pairs={{0,24},{8,16},{16,8},{24,0},{1,25},{9,17},{17,9},{25,1},{2,26},{10... | collective-permute-start | bytes 786440 | tf_op jit(solution)/shard_map/ppermute | solution.py:18
  133.6 89.3 %all-to-all-start.1 = ((f32[16,16,1024]{2,1,0:T(8,128)}), f32[16,16,1024]{2,1,0:T(8,128)}, u32[]{:S(2)}, u32[]{:S(2)}) async-start(f32[16,16,1024]{2,1,0:T(8,128)} %fusion.6), calls=%async_computation.1 | async-start | bytes 2097152 | tf_op jit(solution)/shard_map/all_to_all | solution.py:13
  147.5 4.8 %collective-permute-start = (f32[512,256]{1,0:T(8,128)S(1)}, f32[512,256]{1,0:T(8,128)S(1)}, u32[]{:S(2)}, u32[]{:S(2)}) collective-permute-start(f32[512,256]{1,0:T(8,128)S(1)} %constant_dynamic-slice_fusion.8), channel_id=1, source_target_pairs={{0,1},{1,0},{2,3},{3,2},{4,5},{5,4},{6,7},{7,6},{8,9},{9,8},{10,11... | collective-permute-start | bytes 1572872 | tf_op jit(solution)/shard_map/ppermute | solution.py:18
  152.4 9.8 %collective-permute-start.1 = (f32[4,32,256]{2,1,0:T(8,128)S(1)}, f32[4,32,256]{2,1,0:T(8,128)S(1)}, u32[]{:S(2)}, u32[]{:S(2)}) collective-permute-start(f32[4,32,256]{2,1,0:T(8,128)S(1)} %get-tuple-element.12), channel_id=1, source_target_pairs={{0,32},{32,0},{64,96},{96,64},{1,33},{33,1},{65,97},{97,65},{2,34}... | collective-permute-start | bytes 393224 | tf_op jit(solution)/shard_map/ppermute | solution.py:18
  155.9 9.2 %collective-permute-start.2 = (f32[4,32,256]{2,1,0:T(8,128)S(1)}, f32[4,32,256]{2,1,0:T(8,128)S(1)}, u32[]{:S(2)}, u32[]{:S(2)}) collective-permute-start(f32[4,32,256]{2,1,0:T(8,128)S(1)} %get-tuple-element.11), channel_id=1, source_target_pairs={{0,64},{32,96},{64,0},{96,32},{1,65},{33,97},{65,1},{97,33},{2,66}... | collective-permute-start | bytes 393224 | tf_op jit(solution)/shard_map/ppermute | solution.py:18
  160.2 7.3 %collective-permute-start.3 = (f32[4,32,256]{2,1,0:T(8,128)S(1)}, f32[4,32,256]{2,1,0:T(8,128)S(1)}, u32[]{:S(2)}, u32[]{:S(2)}) collective-permute-start(f32[4,32,256]{2,1,0:T(8,128)S(1)} %get-tuple-element.10), channel_id=1, source_target_pairs={{0,96},{32,64},{64,32},{96,0},{1,97},{33,65},{65,33},{97,1},{2,98}... | collective-permute-start | bytes 393224 | tf_op jit(solution)/shard_map/ppermute | solution.py:18
  179.8 16.2 %collective-permute-start.4 = (f32[32,256]{1,0:T(8,128)S(1)}, f32[32,256]{1,0:T(8,128)S(1)}, u32[]{:S(2)}, u32[]{:S(2)}) collective-permute-start(f32[32,256]{1,0:T(8,128)S(1)} %get-tuple-element.23), channel_id=1, source_target_pairs={{0,128},{128,0},{256,384},{384,256},{1,129},{129,1},{257,385},{385... | collective-permute-start | bytes 98312 | tf_op jit(solution)/shard_map/ppermute | solution.py:18
  186.9 13.4 %collective-permute-start.5 = (f32[32,256]{1,0:T(8,128)S(1)}, f32[32,256]{1,0:T(8,128)S(1)}, u32[]{:S(2)}, u32[]{:S(2)}) collective-permute-start(f32[32,256]{1,0:T(8,128)S(1)} %get-tuple-element.22), channel_id=1, source_target_pairs={{0,256},{128,384},{256,0},{384,128},{1,257},{129,385},{257,1},{385... | collective-permute-start | bytes 98312 | tf_op jit(solution)/shard_map/ppermute | solution.py:18
  193.9 8.9 %collective-permute-start.6 = (f32[32,256]{1,0:T(8,128)S(1)}, f32[32,256]{1,0:T(8,128)S(1)}, u32[]{:S(2)}, u32[]{:S(2)}) collective-permute-start(f32[32,256]{1,0:T(8,128)S(1)} %get-tuple-element.21), channel_id=1, source_target_pairs={{0,384},{128,256},{256,128},{384,0},{1,385},{129,257},{257,129},{3... | collective-permute-start | bytes 98312 | tf_op jit(solution)/shard_map/ppermute | solution.py:18
